TPU v7x, 256 devices: a whole 4x4x8 slice. The times are simulated.
256 devices in a mesh: tm: 16 (over y, x), space: 16 (over z, core).
Axes of the slice: x: 4, y: 4, z: 8, core: 2. Of those that a mesh axis runs over, the one named last changes fastest.
Arguments:
- starts: float32 [16, 3, 128, 64, 128], P('tm', None, 'space'), may hold values from -6 to 6
- strain: bfloat16 [16, 9, 128, 64, 128], P('tm', None, 'space'), may hold values from -0.59765625 to 0.59765625
Outputs:
- corrected: float32 [16, 3, 128, 64, 128], P('tm', None, 'space')
All inputs are finite; a program needn't handle non-finite values.
Results may differ from a plain program's by a relative error of at most 0.0003.
Values sent between devices are 32-bit elements; how exact they have to be, the bound alone decides.
No kernel may reach another device: no remote copies, remote signals or barrier semaphores. Data moves between devices by JAX's collectives and lax.ppermute only.
A program may use at most 128 MiB of HBM per device.

v0:
```python
import jax
import jax.numpy as jnp
from jax import lax
from jax.sharding import PartitionSpec as P

COARSEN = 4


kernel_near = 0.8
kernel_far = 0.2
diffusion = 0.08
coarse_rate = 0.1


def padded_2(cells, sides, width):
    for axis, dim in sides:
        count = lax.axis_size(axis)
        ends = count - 1
        head = lax.slice_in_dim(cells, 0, width, axis=dim)
        tail = lax.slice_in_dim(cells, cells.shape[dim] - width, cells.shape[dim], axis=dim)
        cells = jnp.concatenate(
            [
                lax.ppermute(tail, axis, [(i, (i + 1) % count) for i in range(ends)]),
                cells,
                lax.ppermute(head, axis, [((i + 1) % count, i) for i in range(ends)]),
            ],
            axis=dim,
        )
    return cells


def passed_along(block, axis, distance):
    devices = range(lax.axis_size(axis))
    route = [(i - distance, i) for i in devices if i - distance in devices]
    return lax.ppermute(block, axis, route)


def depth_terms(padded, field, depth):
    near_sum = padded[:, 3 : 3 + depth] + padded[:, 1 : 1 + depth] - 2.0 * field
    far_sum = padded[:, 4 : 4 + depth] + padded[:, 0:depth] - 2.0 * field
    return kernel_near * near_sum + kernel_far * far_sum


def plane_terms(field):
    total = jnp.zeros_like(field)
    for along in (2, 3):
        near_sum = jnp.roll(field, 1, along) + jnp.roll(field, -1, along) - 2.0 * field
        far_sum = jnp.roll(field, 2, along) + jnp.roll(field, -2, along) - 2.0 * field
        total = total + kernel_near * near_sum + kernel_far * far_sum
    return total


def stretch_terms(field, strain):
    result = []
    for row in range(3):
        acc = strain[3 * row].astype(jnp.float32) * field[0]
        acc = acc + strain[3 * row + 1].astype(jnp.float32) * field[1]
        acc = acc + strain[3 * row + 2].astype(jnp.float32) * field[2]
        result.append(acc)
    return jnp.stack(result, axis=0)


def restrict_field(field):
    comps, depth, width_x, width_y = field.shape
    blocks = field.reshape(
        comps, depth // COARSEN, COARSEN, width_x // COARSEN, COARSEN, width_y // COARSEN, COARSEN
    )
    return jnp.mean(blocks, axis=(2, 4, 6))


def prolong_field(coarse):
    comps, depth, width_x, width_y = coarse.shape
    spread = jnp.broadcast_to(
        coarse[:, :, None, :, None, :, None],
        (comps, depth, COARSEN, width_x, COARSEN, width_y, COARSEN),
    )
    return spread.reshape(comps, depth * COARSEN, width_x * COARSEN, width_y * COARSEN)


def coarse_step(field, padded):
    near_sum = padded[..., 2:, :, :] + padded[..., :-2, :, :]
    near_sum = near_sum + jnp.roll(field, 1, -2) + jnp.roll(field, -1, -2)
    near_sum = near_sum + jnp.roll(field, 1, -1) + jnp.roll(field, -1, -1)
    return field + coarse_rate * (near_sum - 6.0 * field)


def coarse_apply(field):
    padded = padded_2(field, (("space", 1),), 1)
    return coarse_step(field, padded)


def solve_small(factor, vector):
    lower = lax.linalg.triangular_solve(factor, vector[:, None], left_side=True, lower=True)
    upper = lax.linalg.triangular_solve(factor, lower, left_side=True, lower=True, transpose_a=True)
    return upper[:, 0]


def local(starts, strain):
    field = starts[0]
    depth = field.shape[1]
    padded = padded_2(field, (("space", 1),), 2)
    depth_part = depth_terms(padded, field, depth)
    fine_ends = (
        field + stretch_terms(field, strain[0]) + diffusion * (depth_part + plane_terms(field))
    )
    start_coarse = restrict_field(field)
    end_coarse = restrict_field(fine_ends)
    slices = lax.axis_size("tm")
    slice_index = lax.axis_index("tm")
    snap_basis, images = (
        lax.all_gather(start_coarse[None], "tm", axis=0, tiled=True),
        lax.all_gather(end_coarse[None], "tm", axis=0, tiled=True),
    )
    flat_basis = snap_basis.reshape(slices, -1)
    flat_images = images.reshape(slices, -1)
    local_gram = jnp.dot(flat_basis, flat_basis.T, precision=lax.Precision.HIGHEST)
    gram_matrix = lax.psum(local_gram, "space")
    factor = jnp.linalg.cholesky(gram_matrix)
    shape = start_coarse.shape

    def kapply(gap):
        product = jnp.dot(flat_basis, gap.reshape(-1), precision=lax.Precision.HIGHEST)
        coeffs = solve_small(factor, lax.psum(product, "space"))
        spanned = jnp.dot(coeffs, flat_images, precision=lax.Precision.HIGHEST).reshape(shape)
        remainder = gap - jnp.dot(coeffs, flat_basis, precision=lax.Precision.HIGHEST).reshape(
            shape
        )
        return spanned + coarse_apply(remainder)

    def advance(counter, carried):
        incoming = passed_along(end_coarse + carried, "tm", 1)
        gap = jnp.where(slice_index == 0, jnp.zeros_like(incoming), incoming - start_coarse)
        return kapply(gap)

    carried = lax.fori_loop(0, slices - 1, advance, jnp.zeros(shape, jnp.float32))
    corrected = fine_ends + prolong_field(carried)
    return corrected[None]


def solution(mesh):
    return jax.shard_map(
        local,
        mesh=mesh,
        in_specs=(P("tm", None, "space", None, None), P("tm", None, "space", None, None)),
        out_specs=P("tm", None, "space", None, None),
        check_vma=False,
    )
```

profile of v0, /device:TPU:105, one launch (start us, length us, event | category | flops | bytes accessed | tf_op | source)
XLA Modules:
  0.0 867.9 jit_solution(10623988126440939948)
XLA Ops:
  27.3 28.1 %reshape_squeeze.3 = f32[3,2,4,16,4,32,4]{6,5,4,3,2,1,0:T(8,128)} reshape(f32[1,3,8,64,128]{4,3,2,1,0:T(8,128)} %param.4) | data formatting | bytes 1572864 | tf_op jit(solution)/shard_map/reshape;squeeze | solution.py:65
  57.8 9.6 %reduce_sum.18 = f32[3,2,16,32]{3,2,1,0:T(8,128)S(1)} reduce(f32[3,2,4,16,4,32,4]{6,5,4,3,2,1,0:T(8,128)} %reshape_squeeze.3, f32[]{:T(128)} %constant.83.clone.1), dimensions={2,4,6}, to_apply=%region_1.2 | reduce | flops 193536 | bytes 798724 | tf_op jit(solution)/shard_map/reduce_sum | solution.py:68
  67.4 19.4 %all-gather = f32[48,2,16,32]{3,2,1,0:T(8,128)S(1)} all-gather(f32[3,2,16,32]{3,2,1,0:T(8,128)S(1)} %broadcast_multiply_fusion.1), channel_id=2, replica_groups=mesh['tm'=16,'space'=16] {'tm'}, dimensions={0}, use_global_device_ids=true | all-gather | bytes 208896 | tf_op jit(solution)/shard_map/all_gather | solution.py:111
  88.6 26.4 %psum.16 = f32[16,16]{0,1:T(8,128)S(1)} all-reduce(f32[16,16]{0,1:T(8,128)S(1)} %convolution_bitcast_fusion.3), channel_id=1, replica_groups=mesh['tm'=16,'space'=16] {'space'}, use_global_device_ids=true, to_apply=%region_2.3 | all-reduce | flops 256 | bytes 2048 | tf_op jit(solution)/shard_map/psum | solution.py:117
  122.8 27.3 %reshape.334 = f32[3,2,4,16,4,32,4]{6,5,4,3,2,1,0:T(8,128)} reshape(f32[3,8,64,128]{3,2,1,0:T(8,128)S(1)} %fusion.19) | data formatting | bytes 1572864 | tf_op jit(solution)/shard_map/reshape | solution.py:65
  159.7 18.2 %all-gather.1 = f32[48,2,16,32]{3,2,1,0:T(8,128)S(1)} all-gather(f32[3,2,16,32]{3,2,1,0:T(8,128)S(1)} %broadcast_multiply_fusion), channel_id=3, replica_groups=mesh['tm'=16,'space'=16] {'tm'}, dimensions={0}, use_global_device_ids=true | all-gather | bytes 208896 | tf_op jit(solution)/shard_map/all_gather | solution.py:112
  178.3 655.6 %while.13 = (s32[]{:T(128)}, f32[3,2,16,32]{3,2,1,0:T(8,128)S(1)}, f32[16,16]{1,0:T(8,128)S(1)}, pred[]{:T(512)}, f32[3,2,16,32]{3,2,1,0:T(8,128)S(1)}, /*index=...) while((s32[]{:T(128)}, f32[3,2,16,32]{3,2,1,0:T(8,128)S(1)}, ...), condition=%wide.region_7.8_spmd.clone, body=%wide.region_5.7_spmd.clone.sunk | while | flops 1840659 | bytes 1135400 | solution.py:135
  185.6 29.4 %psum.19 = f32[16]{0:T(128)S(1)} all-reduce(f32[16]{0:T(128)S(1)} %convolution_bitcast_fusion.7), channel_id=1, replica_groups=mesh['tm'=16,'space'=16] {'space'}, use_global_device_ids=true, to_apply=%region_6.6 | all-reduce | flops 16 | bytes 128 | tf_op jit(solution)/shard_map/while/body/eval_jaxpr/psum | solution.py:123
  235.3 23.0 %psum.19 = f32[16]{0:T(128)S(1)} all-reduce(f32[16]{0:T(128)S(1)} %convolution_bitcast_fusion.7), channel_id=1, replica_groups=mesh['tm'=16,'space'=16] {'space'}, use_global_device_ids=true, to_apply=%region_6.6 | all-reduce | flops 16 | bytes 128 | tf_op jit(solution)/shard_map/while/body/eval_jaxpr/psum | solution.py:123
  278.6 23.0 %psum.19 = f32[16]{0:T(128)S(1)} all-reduce(f32[16]{0:T(128)S(1)} %convolution_bitcast_fusion.7), channel_id=1, replica_groups=mesh['tm'=16,'space'=16] {'space'}, use_global_device_ids=true, to_apply=%region_6.6 | all-reduce | flops 16 | bytes 128 | tf_op jit(solution)/shard_map/while/body/eval_jaxpr/psum | solution.py:123
  321.9 23.0 %psum.19 = f32[16]{0:T(128)S(1)} all-reduce(f32[16]{0:T(128)S(1)} %convolution_bitcast_fusion.7), channel_id=1, replica_groups=mesh['tm'=16,'space'=16] {'space'}, use_global_device_ids=true, to_apply=%region_6.6 | all-reduce | flops 16 | bytes 128 | tf_op jit(solution)/shard_map/while/body/eval_jaxpr/psum | solution.py:123
  365.2 23.0 %psum.19 = f32[16]{0:T(128)S(1)} all-reduce(f32[16]{0:T(128)S(1)} %convolution_bitcast_fusion.7), channel_id=1, replica_groups=mesh['tm'=16,'space'=16] {'space'}, use_global_device_ids=true, to_apply=%region_6.6 | all-reduce | flops 16 | bytes 128 | tf_op jit(solution)/shard_map/while/body/eval_jaxpr/psum | solution.py:123
  408.4 23.0 %psum.19 = f32[16]{0:T(128)S(1)} all-reduce(f32[16]{0:T(128)S(1)} %convolution_bitcast_fusion.7), channel_id=1, replica_groups=mesh['tm'=16,'space'=16] {'space'}, use_global_device_ids=true, to_apply=%region_6.6 | all-reduce | flops 16 | bytes 128 | tf_op jit(solution)/shard_map/while/body/eval_jaxpr/psum | solution.py:123
  451.7 23.0 %psum.19 = f32[16]{0:T(128)S(1)} all-reduce(f32[16]{0:T(128)S(1)} %convolution_bitcast_fusion.7), channel_id=1, replica_groups=mesh['tm'=16,'space'=16] {'space'}, use_global_device_ids=true, to_apply=%region_6.6 | all-reduce | flops 16 | bytes 128 | tf_op jit(solution)/shard_map/while/body/eval_jaxpr/psum | solution.py:123
  495.0 23.0 %psum.19 = f32[16]{0:T(128)S(1)} all-reduce(f32[16]{0:T(128)S(1)} %convolution_bitcast_fusion.7), channel_id=1, replica_groups=mesh['tm'=16,'space'=16] {'space'}, use_global_device_ids=true, to_apply=%region_6.6 | all-reduce | flops 16 | bytes 128 | tf_op jit(solution)/shard_map/while/body/eval_jaxpr/psum | solution.py:123
  538.3 23.0 %psum.19 = f32[16]{0:T(128)S(1)} all-reduce(f32[16]{0:T(128)S(1)} %convolution_bitcast_fusion.7), channel_id=1, replica_groups=mesh['tm'=16,'space'=16] {'space'}, use_global_device_ids=true, to_apply=%region_6.6 | all-reduce | flops 16 | bytes 128 | tf_op jit(solution)/shard_map/while/body/eval_jaxpr/psum | solution.py:123
  581.6 23.0 %psum.19 = f32[16]{0:T(128)S(1)} all-reduce(f32[16]{0:T(128)S(1)} %convolution_bitcast_fusion.7), channel_id=1, replica_groups=mesh['tm'=16,'space'=16] {'space'}, use_global_device_ids=true, to_apply=%region_6.6 | all-reduce | flops 16 | bytes 128 | tf_op jit(solution)/shard_map/while/body/eval_jaxpr/psum | solution.py:123
  624.9 23.0 %psum.19 = f32[16]{0:T(128)S(1)} all-reduce(f32[16]{0:T(128)S(1)} %convolution_bitcast_fusion.7), channel_id=1, replica_groups=mesh['tm'=16,'space'=16] {'space'}, use_global_device_ids=true, to_apply=%region_6.6 | all-reduce | flops 16 | bytes 128 | tf_op jit(solution)/shard_map/while/body/eval_jaxpr/psum | solution.py:123
  668.1 23.0 %psum.19 = f32[16]{0:T(128)S(1)} all-reduce(f32[16]{0:T(128)S(1)} %convolution_bitcast_fusion.7), channel_id=1, replica_groups=mesh['tm'=16,'space'=16] {'space'}, use_global_device_ids=true, to_apply=%region_6.6 | all-reduce | flops 16 | bytes 128 | tf_op jit(solution)/shard_map/while/body/eval_jaxpr/psum | solution.py:123
  711.4 23.0 %psum.19 = f32[16]{0:T(128)S(1)} all-reduce(f32[16]{0:T(128)S(1)} %convolution_bitcast_fusion.7), channel_id=1, replica_groups=mesh['tm'=16,'space'=16] {'space'}, use_global_device_ids=true, to_apply=%region_6.6 | all-reduce | flops 16 | bytes 128 | tf_op jit(solution)/shard_map/while/body/eval_jaxpr/psum | solution.py:123
  754.7 23.0 %psum.19 = f32[16]{0:T(128)S(1)} all-reduce(f32[16]{0:T(128)S(1)} %convolution_bitcast_fusion.7), channel_id=1, replica_groups=mesh['tm'=16,'space'=16] {'space'}, use_global_device_ids=true, to_apply=%region_6.6 | all-reduce | flops 16 | bytes 128 | tf_op jit(solution)/shard_map/while/body/eval_jaxpr/psum | solution.py:123
  798.0 23.0 %psum.19 = f32[16]{0:T(128)S(1)} all-reduce(f32[16]{0:T(128)S(1)} %convolution_bitcast_fusion.7), channel_id=1, replica_groups=mesh['tm'=16,'space'=16] {'space'}, use_global_device_ids=true, to_apply=%region_6.6 | all-reduce | flops 16 | bytes 128 | tf_op jit(solution)/shard_map/while/body/eval_jaxpr/psum | solution.py:123
  833.9 11.6 %broadcast_in_dim.7 = f32[3,2,4,16,4,32,4]{6,5,4,3,2,1,0:T(8,128)} broadcast(f32[3,2,16,32]{3,2,1,0:T(8,128)S(1)} %get-tuple-element.99), dimensions={0,1,3,5} | broadcast | bytes 798720 | tf_op jit(solution)/shard_map/broadcast_in_dim | solution.py:73
  845.5 21.4 %reshape.337 = f32[3,8,64,128]{3,2,1,0:T(8,128)S(1)} reshape(f32[3,2,4,16,4,32,4]{6,5,4,3,2,1,0:T(8,128)} %broadcast_in_dim.7) | data formatting | bytes 1572864 | tf_op jit(solution)/shard_map/reshape | solution.py:77
  (406 shorter events, 352.0 us)
Async XLA Ops:
  1.9 115.9 %collective-permute-start.3 = (f32[3,2,64,128]{3,2,1,0:T(8,128)}, f32[3,2,64,128]{3,2,1,0:T(8,128)}, u32[]{:S(2)}, u32[]{:S(2)}) collective-permute-start(f32[3,2,64,128]{3,2,1,0:T(8,128)} %get-tuple-element.172), channel_id=1, source_target_pairs={{1,0},{2,1},{3,2},{4,3},{5,4},{6,5},{7,6},{8,7},{9,8},{10,9},{11,1... | collective-permute-start | bytes 589832 | tf_op jit(solution)/shard_map/ppermute | solution.py:25
  4.5 113.4 %collective-permute-start.4 = (f32[3,2,64,128]{3,2,1,0:T(8,128)}, f32[3,2,64,128]{3,2,1,0:T(8,128)}, u32[]{:S(2)}, u32[]{:S(2)}) collective-permute-start(f32[3,2,64,128]{3,2,1,0:T(8,128)} %get-tuple-element.173), channel_id=1, source_target_pairs={{0,1},{1,2},{2,3},{3,4},{4,5},{5,6},{6,7},{7,8},{8,9},{9,10},{10,1... | collective-permute-start | bytes 589832 | tf_op jit(solution)/shard_map/ppermute | solution.py:23
  178.3 6.9 collective-permute-start
  216.1 7.4 collective-permute-start.1
  228.0 6.9 collective-permute-start
  259.4 7.4 collective-permute-start.1
  271.3 6.9 collective-permute-start
  302.7 7.4 collective-permute-start.1
  314.6 6.9 collective-permute-start
  345.9 7.4 collective-permute-start.1
  357.8 6.9 collective-permute-start
  389.2 7.4 collective-permute-start.1
  401.1 6.9 collective-permute-start
  432.5 7.4 collective-permute-start.1
  444.4 6.9 collective-permute-start
  475.8 7.4 collective-permute-start.1
  519.1 7.4 collective-permute-start.1
  562.4 7.4 collective-permute-start.1
  605.6 7.4 collective-permute-start.1
  648.9 7.4 collective-permute-start.1
  692.2 7.4 collective-permute-start.1
  735.5 7.4 collective-permute-start.1
  778.8 7.4 collective-permute-start.1
  822.1 7.4 collective-permute-start.1
  (24 other events, 206.3 us)
where the time goes:
time: 870 us; the launch traced here: 868 us
  blocking collectives  416 us (48%)
  starting transfers between devices  146 us (17%)
  waiting for transfers between devices  121 us (14%)
  local copies, waits for them, and re-layouts  116 us (13%)
  other arithmetic  50.7 us (6%)
  matrix products  16.3 us (2%)
    psum x15, blocking collectives, kapply(): coeffs = solve_small(factor, lax.psum(product, 'space'))  352 us
    ppermute x16, starting transfers between devices, padded_2(): lax.ppermute(tail, axis, [(i, (i + 1) % count) for i in range(ends)])  85.6 us
    ppermute x16, waiting for transfers between devices, padded_2(): lax.ppermute(head, axis, [((i + 1) % count, i) for i in range(ends)])  65 us
    ppermute x15, waiting for transfers between devices, passed_along(): return lax.ppermute(block, axis, route)  56.1 us
    ppermute x16, starting transfers between devices, padded_2(): lax.ppermute(head, axis, [((i + 1) % count, i) for i in range(ends)])  31.4 us
    ppermute x15, starting transfers between devices, passed_along(): return lax.ppermute(block, axis, route)  29.4 us
    another operation x1, local copies, waits for them, and re-layouts, restrict_field(): field.reshape(comps, depth // COARSEN, COARSEN, width_x // COARSEN, COARS...  28.1 us
    reshape x1, local copies, waits for them, and re-layouts, restrict_field(): field.reshape(comps, depth // COARSEN, COARSEN, width_x // COARSEN, COARS...  27.3 us
  transfers between devices with their start and end apart: 47, of which 30 were waited for; matrix products, arithmetic and copies ran while one was open for 10% of the time, Pallas kernels for 0%

commit v1 on v0

v1 whole, which is shorter than its diff:
```python
import functools

import jax
import jax.numpy as jnp
import numpy as np
from jax import lax
from jax.experimental import pallas as pl
from jax.experimental.pallas import tpu as pltpu
from jax.sharding import PartitionSpec as P

COARSEN = 4
SLICES = 16
DEVICES_Z = 16
NX, NY, NZ = 16, 32, 32
CX, CY = 64, 128
DEPTH = 8

kernel_near = 0.8
kernel_far = 0.2
diffusion = 0.08
coarse_rate = 0.1

ROWS = 24
HIGH = lax.Precision.HIGHEST


def real_fourier(n):
    x = np.arange(n)
    rows, freq = [np.full(n, 1.0 / np.sqrt(n))], [0]
    for k in range(1, n // 2):
        rows.append(np.sqrt(2.0 / n) * np.cos(2 * np.pi * k * x / n))
        rows.append(np.sqrt(2.0 / n) * np.sin(2 * np.pi * k * x / n))
        freq += [k, k]
    rows.append(((-1.0) ** x) / np.sqrt(n))
    freq.append(n // 2)
    return np.stack(rows), 2 * np.cos(2 * np.pi * np.array(freq) / n)


def constants():
    fx, ex = real_fourier(NX)
    fy, ey = real_fourier(NY)
    k = np.arange(1, NZ + 1)
    sz = np.sqrt(2.0 / (NZ + 1)) * np.sin(np.pi * np.outer(k, k) / (NZ + 1))
    ez = 2 * np.cos(np.pi * k / (NZ + 1))
    spread_x = np.repeat(np.eye(NX), COARSEN, axis=0)
    spread_y = np.repeat(np.eye(NY), COARSEN, axis=0)
    fwd_x = fx @ spread_x.T / 16.0
    fwd_y = spread_y @ fy.T / 4.0
    inv_x = spread_x @ fx.T
    inv_y = fy @ spread_y.T
    wide_fwd_y = np.zeros((3 * CY, 128))
    wide_inv_y = np.zeros((128, 3 * CY))
    for c in range(3):
        wide_fwd_y[c * CY : (c + 1) * CY, 32 * c : 32 * c + 32] = fwd_y
        wide_inv_y[32 * c : 32 * c + 32, c * CY : (c + 1) * CY] = inv_y
    fwd_z = np.zeros((2 * NZ, DEVICES_Z, 8))
    inv_z = np.zeros((DEVICES_Z, 8, NZ))
    for s in range(DEVICES_Z):
        for q in range(2):
            fwd_z[:NZ, s, q] = sz[:, 2 * s + q]
            fwd_z[NZ:, s, 2 + q] = sz[:, 2 * s + q]
            inv_z[s, q] = sz[2 * s + q]
        if s > 0:
            fwd_z[NZ:, s, 4] = sz[:, 2 * s - 1]
        if s < DEVICES_Z - 1:
            fwd_z[NZ:, s, 5] = sz[:, 2 * s + 2]
    full = 1.0 + coarse_rate * (ez[:, None] + ey[None, :] - 6.0)
    packed = np.zeros((ROWS, 128))
    for c in range(3):
        packed[:, 32 * c : 32 * c + 32] = full[:ROWS]
        packed[8 * c : 8 * c + 8, 96:] = full[ROWS:]
    f = lambda a: np.asarray(a, np.float32)
    return dict(
        fwd_x=f(fwd_x),
        wide_fwd_y=f(wide_fwd_y),
        inv_x=f(inv_x),
        wide_inv_y=f(wide_inv_y),
        fwd_z=f(fwd_z.reshape(2 * NZ, DEVICES_Z * 8)),
        inv_z=f(inv_z.reshape(DEVICES_Z * 8, NZ)),
        lam=f(packed),
        lam_full=f(np.tile(full, (1, 4))),
        lam_x=f(coarse_rate * ex),
    )


def dot(a, b, dims=((1,), (0,))):
    return lax.dot_general(
        a, b, (dims, ((), ())), precision=HIGH, preferred_element_type=jnp.float32
    )


def iota(shape, dim):
    return lax.broadcasted_iota(jnp.int32, shape, dim)


def fine_kernel(field_ref, strain_ref, fwd_x_ref, fwd_y_ref, fine_ref, coarse_ref, sums):
    sums[...] = jnp.zeros_like(sums)
    near = diffusion * kernel_near
    far = diffusion * kernel_far
    centre = 1.0 - 6.0 * (near + far)

    def plane(z, _):
        block = z // COARSEN
        up1, up2 = jnp.minimum(z + 1, DEPTH - 1), jnp.minimum(z + 2, DEPTH - 1)
        dn1, dn2 = jnp.maximum(z - 1, 0), jnp.maximum(z - 2, 0)
        w_up1 = jnp.where(z + 1 < DEPTH, near, 0.0).astype(jnp.float32)
        w_up2 = jnp.where(z + 2 < DEPTH, far, 0.0).astype(jnp.float32)
        w_dn1 = jnp.where(z >= 1, near, 0.0).astype(jnp.float32)
        w_dn2 = jnp.where(z >= 2, far, 0.0).astype(jnp.float32)
        comps = [field_ref[c, z] for c in range(3)]
        for c in range(3):
            f = comps[c]
            near_sum = pltpu.roll(f, 1, 0) + pltpu.roll(f, CX - 1, 0)
            near_sum = near_sum + pltpu.roll(f, 1, 1) + pltpu.roll(f, CY - 1, 1)
            far_sum = pltpu.roll(f, 2, 0) + pltpu.roll(f, CX - 2, 0)
            far_sum = far_sum + pltpu.roll(f, 2, 1) + pltpu.roll(f, CY - 2, 1)
            acc = centre * f + near * near_sum + far * far_sum
            acc = acc + w_up1 * field_ref[c, up1] + w_dn1 * field_ref[c, dn1]
            acc = acc + w_up2 * field_ref[c, up2] + w_dn2 * field_ref[c, dn2]
            for j in range(3):
                acc = acc + strain_ref[3 * c + j, z].astype(jnp.float32) * comps[j]
            fine_ref[c, z] = acc
            lanes = slice(c * CY, (c + 1) * CY)
            sums[block, :, lanes] += f
            sums[2 + block, :, lanes] += acc
        return 0

    lax.fori_loop(0, DEPTH, plane, 0)
    for c in range(3):
        lanes = slice(c * CY, (c + 1) * CY)
        sums[4, :, lanes] = diffusion * field_ref[c, 0] + far * field_ref[c, 1]
        sums[5, :, lanes] = diffusion * field_ref[c, DEPTH - 1] + far * field_ref[c, DEPTH - 2]
    along_x = [dot(fwd_x_ref[...], sums[q]) for q in range(6)]
    modes = dot(jnp.concatenate(along_x, axis=0), fwd_y_ref[...])
    for q in range(6):
        coarse_ref[:, q, :] = modes[NX * q : NX * (q + 1)]
    for q in range(6, 8):
        coarse_ref[:, q, :] = jnp.zeros((NX, 128), jnp.float32)


def depth_kernel(modes_ref, fwd_z_ref, lam_ref, lam_x_ref, out_ref):
    lam = lam_ref[...] + lam_x_ref[lax.axis_index("space")]
    both = dot(fwd_z_ref[...], modes_ref[...])
    basis = both[:NZ]
    defect = both[NZ:] - lam * basis
    group = iota((8, 128), 1) // 32
    tiles = []
    for v in (basis, defect):
        rest = v[ROWS:]
        for c in range(3):
            moved = pltpu.roll(rest, 96 - 32 * c, 1)
            tiles.append(jnp.where(group == 3, moved, v[8 * c : 8 * c + 8]))
    packed = jnp.concatenate(tiles, axis=0)
    for m in range(SLICES):
        out_ref[m] = packed


def gram_kernel(all_ref, lam_ref, lam_x_ref, out_ref):
    shift = lam_x_ref[lax.axis_index("space")]
    sub = iota((8, 128), 0)
    total = jnp.zeros((64, 88), jnp.float32)
    for r in range(0, ROWS, 2):
        left, right = [], []
        for row in (r, r + 1):
            b = all_ref[pl.ds(row, SLICES, stride=2 * ROWS), :]
            d = all_ref[pl.ds(ROWS + row, SLICES, stride=2 * ROWS), :]
            lam = lam_ref[row : row + 1, :] + shift
            lam2 = lam * lam
            lam4 = lam2 * lam2
            lam3 = lam2 * lam
            first = d[0:1] + lam * b[0:1]
            powers = jnp.where(sub == 0, 1.0, jnp.where(sub == 1, lam, jnp.where(sub == 2, lam2, lam3)))
            b4 = b * lam4
            b8 = b4 * lam4
            left.append(jnp.concatenate([b, b4, b8, b8 * lam4], axis=0))
            right.append(
                jnp.concatenate([d, d * lam, d * lam2, d * lam3, b, powers * first], axis=0)
            )
        total = total + dot(
            jnp.concatenate(left, axis=1), jnp.concatenate(right, axis=1), ((1,), (1,))
        )
    total = jnp.concatenate([total, jnp.zeros((64, 40), jnp.float32)], axis=1)
    a = [total[16 * i : 16 * i + 16] for i in range(4)]
    lane = iota((16, 128), 1)
    low = jnp.where(lane < 64, a[0], pltpu.roll(a[1], 64, 1))
    high = jnp.where(lane < 64, a[2], pltpu.roll(a[3], 64, 1))
    high = jnp.where((lane >= 96) & (lane < 112), pltpu.roll(a[0], 32, 1), high)
    for i in range(4):
        at = 112 + 4 * i
        high = jnp.where((lane >= at) & (lane < at + 4), pltpu.roll(a[i], (at - 80) % 128, 1), high)
    out_ref[:, :128] = low
    out_ref[:, 128:] = high


def solve_kernel(sums_ref, all_ref, inv_z_ref, lam_ref, lam_x_ref, out_ref):
    shift = lam_x_ref[lax.axis_index("space")]
    slice_index = lax.axis_index("tm")
    parts = sums_ref.shape[0]
    total = sums_ref[0]
    for i in range(1, parts):
        total = total + sums_ref[i]
    low, high = total[:, :128], total[:, 128:]
    lane = iota((16, 128), 1)
    sub = iota((16, 128), 0)
    for i in range(SLICES):
        column = high[:, 96 + i : 97 + i]
        scale = 1.0 / column[i : i + 1]
        factor = jnp.where(sub[:, :1] == i, column - 1.0, column) * scale
        low, high = low - factor * low[i : i + 1], high - factor * high[i : i + 1]
    diag = (lane & 15) == sub
    spread = (lane >> 3) == sub
    block = (iota((8, 128), 1) & 7) == iota((8, 128), 0)
    h_high = jnp.where(lane < 96, high, 0.0)
    acc_low = jnp.zeros((16, 128), jnp.float32)
    acc_high = jnp.zeros((16, 128), jnp.float32)
    first = jnp.where(iota((1, 128), 1) < 8, 1.0, 0.0)
    weights = [jnp.where(block, first, 0.0)]
    for k in range(1, SLICES):
        at = jnp.where(lane < 16, acc_low, 0.0) + jnp.where(lane == 112 + k - 1, high, 0.0)
        c = jnp.sum(at, axis=1, keepdims=True)
        weights.append(
            jnp.where(block, jnp.sum(jnp.where(spread, c, 0.0), axis=0, keepdims=True), 0.0)
        )
        if k < SLICES - 1:
            row = jnp.sum(jnp.where(diag, c, 0.0), axis=0, keepdims=True)
            shifted_low, shifted_high = pltpu.roll(acc_low, 112, 1), pltpu.roll(acc_high, 112, 1)
            if k > 1:
                acc_low = jnp.where(lane < 112, shifted_low, shifted_high)
                acc_high = jnp.where(lane < 112, shifted_high, 0.0)
            acc_low = acc_low + low * row
            acc_high = acc_high + h_high * row
    weights = jnp.concatenate(weights, axis=0)
    tiles = []
    for g in range(3):
        rows = slice(8 * g, 8 * g + 8)
        lam = lam_ref[rows] + shift
        d = all_ref[:, ROWS + 8 * g : ROWS + 8 * g + 8, :].reshape(128, 128)
        terms = dot(weights, d)
        b0 = all_ref[0, rows, :]
        value = terms[0:8] + lam * b0
        for k in range(1, SLICES):
            value = jnp.where(k <= slice_index, lam * value + terms[8 * k : 8 * k + 8], value)
        b_n = all_ref[slice_index, rows, :]
        d_n = all_ref[slice_index, ROWS + 8 * g : ROWS + 8 * g + 8, :]
        tiles.append(value - d_n - lam * b_n)
    group = iota((8, 128), 1) // 32
    rest = jnp.zeros((8, 128), jnp.float32)
    for c in range(3):
        rest = jnp.where(group == c, pltpu.roll(tiles[c], (32 * c - 96) % 128, 1), rest)
    out_ref[...] = dot(inv_z_ref[...], jnp.concatenate(tiles + [rest], axis=0))


def finish_kernel(fine_ref, below_ref, above_ref, modes_ref, inv_x_ref, inv_y_ref, out_ref):
    near = diffusion * kernel_near
    far = diffusion * kernel_far
    for q in range(2):
        along_x = dot(inv_x_ref[...], modes_ref[:, q, :])
        both = dot(along_x, inv_y_ref[...])
        for c in range(3):
            carried = both[:, c * CY : (c + 1) * CY]
            for k in range(COARSEN):
                z = COARSEN * q + k
                value = fine_ref[c, z] + carried
                if z == 0:
                    value = value + near * below_ref[c, 1] + far * below_ref[c, 0]
                if z == 1:
                    value = value + far * below_ref[c, 1]
                if z == DEPTH - 1:
                    value = value + near * above_ref[c, 0] + far * above_ref[c, 1]
                if z == DEPTH - 2:
                    value = value + far * above_ref[c, 0]
                out_ref[c, z] = value


VMEM = pl.BlockSpec(memory_space=pltpu.VMEM)
SMEM = pl.BlockSpec(memory_space=pltpu.SMEM)


def call(kernel, shapes, specs, scratch=()):
    out = jax.tree.map(lambda s: jax.ShapeDtypeStruct(s, jnp.float32), shapes, is_leaf=lambda s: isinstance(s, tuple) and isinstance(s[0], int))
    return pl.pallas_call(
        kernel,
        out_shape=out,
        in_specs=specs,
        out_specs=jax.tree.map(lambda _: VMEM, out),
        scratch_shapes=list(scratch),
    )


def local(starts, strain):
    con = constants()
    field, rates = starts[0], strain[0]
    count = lax.axis_size("space")
    below = lax.ppermute(field[:, DEPTH - 2 :], "space", [(i, i + 1) for i in range(count - 1)])
    above = lax.ppermute(field[:, :2], "space", [(i + 1, i) for i in range(count - 1)])

    fine, coarse = call(
        fine_kernel,
        [(3, DEPTH, CX, CY), (NX, 8, 128)],
        [VMEM] * 4,
        [pltpu.VMEM((6, CX, 3 * CY), jnp.float32)],
    )(field, rates, con["fwd_x"], con["wide_fwd_y"])
    coarse = lax.all_to_all(coarse, "space", 0, 0, tiled=True)
    mine = call(depth_kernel, (SLICES, 2 * ROWS, 128), [VMEM] * 3 + [SMEM])(
        coarse.reshape(128, 128), con["fwd_z"], con["lam_full"], con["lam_x"]
    )
    every = lax.all_to_all(mine, "tm", 0, 0, tiled=True)
    share = call(gram_kernel, (SLICES, 256), [VMEM] * 2 + [SMEM])(
        every.reshape(SLICES * 2 * ROWS, 128), con["lam"], con["lam_x"]
    )
    share = share + lax.ppermute(share, "space", [(i, i ^ 1) for i in range(count)])
    groups = [list(range(0, count, 2)), list(range(1, count, 2))]
    shares = lax.all_to_all(
        jnp.broadcast_to(share[None], (count // 2,) + share.shape),
        "space",
        0,
        0,
        axis_index_groups=groups,
        tiled=True,
    )
    carried = call(solve_kernel, (128, 128), [VMEM] * 4 + [SMEM])(
        shares, every, con["inv_z"], con["lam"], con["lam_x"]
    )
    carried = lax.all_to_all(carried.reshape(DEVICES_Z, 8, 128), "space", 0, 0, tiled=True)
    corrected = call(finish_kernel, (3, DEPTH, CX, CY), [VMEM] * 6)(
        fine, below, above, carried, con["inv_x"], con["wide_inv_y"]
    )
    return corrected[None]


def solution(mesh):
    return jax.shard_map(
        local,
        mesh=mesh,
        in_specs=(P("tm", None, "space", None, None), P("tm", None, "space", None, None)),
        out_specs=P("tm", None, "space", None, None),
        check_vma=False,
    )
```

time: 870 us -> 81.8 us (0.09)
  the two profiles are of different devices: /device:TPU:105 before, /device:TPU:1 now
where the time goes in v1:
time: 81.8 us; the launch traced here: 81.2 us
  blocking collectives  34.3 us (42%)
  Pallas kernels  17.1 us (21%)
  starting transfers between devices  15.5 us (19%)
  waiting for transfers between devices  11.5 us (14%)
  local copies, waits for them, and re-layouts  1.97 us (2%)
    all_to_all x1, blocking collectives, local(): coarse = lax.all_to_all(coarse, 'space', 0, 0, tiled=True)  18 us
    all_to_all x1, blocking collectives, local(): every = lax.all_to_all(mine, 'tm', 0, 0, tiled=True)  16.3 us
    all_to_all x1, waiting for transfers between devices, local(): lax.all_to_all(carried.reshape(DEVICES_Z, 8, 128), 'space', 0, 0, tiled=T...  7.8 us
    pallas_call x1, Pallas kernels, local(): call(solve_kernel, (128, 128), [VMEM] * 4 + [SMEM])  5.07 us
    all_to_all x1, starting transfers between devices, local(): lax.all_to_all(carried.reshape(DEVICES_Z, 8, 128), 'space', 0, 0, tiled=T...  4.87 us
    pallas_call x1, Pallas kernels, local(): call(fine_kernel, [(3, DEPTH, CX, CY), (NX, 8, 128)], [VMEM] * 4, [pltpu....  4.47 us
    ppermute x1, starting transfers between devices, local(): lax.ppermute(field[:, DEPTH - 2:], 'space', [(i, i + 1) for i in range(co...  3.43 us
    all_to_all x1, starting transfers between devices, local(): lax.all_to_all(jnp.broadcast_to(share[None], (count // 2,) + share.shape)...  3.37 us
  transfers between devices with their start and end apart: 5, of which 3 were waited for; matrix products, arithmetic and copies ran while one was open for 0% of the time, Pallas kernels for 6%

profile of v1, /device:TPU:1, one launch (start us, length us, event | category | flops | bytes accessed | tf_op | source)
XLA Modules:
  0.0 81.2 jit_solution(2008449700965133072)
XLA Ops:
  0.0 4.5 %shard_map.109 = (f32[3,8,64,128]{3,2,1,0:T(8,128)}, f32[16,8,128]{2,1,0:T(8,128)}) custom-call(f32[3,8,64,128]{3,2,1,0:T(8,128)} %bitcast.7, bf16[9,8,64,128]{3,2,1,0:T(8,128)(2,1)} %bitcast.9, f32[16,64]{1,0:T(8,128)} %constant.18.clone.fwd_x_ref, f32[384,128]{1,0:T(8,128)} %constant.19.clone.fwd_y_ref), custom_call_target="tpu_custom_call" | custom-call | tf_op jit(solution)/shard_map/pallas_call | solution.py:297
  4.5 18.0 %all_to_all.20 = f32[16,8,128]{2,1,0:T(8,128)} all-to-all(f32[16,8,128]{2,1,0:T(8,128)} %get-tuple-element.8), channel_id=1, replica_groups=mesh['tm'=16,'space'=16] {'space'}, dimensions={0} | all-to-all | bytes 131072 | tf_op jit(solution)/shard_map/all_to_all | solution.py:303
  22.5 1.9 %shard_map.110 = f32[16,48,128]{2,1,0:T(8,128)} custom-call(f32[128,128]{1,0:T(8,128)} %bitcast.11, f32[64,128]{1,0:T(8,128)} %constant.20.clone.fwd_z_ref, f32[32,128]{1,0:T(8,128)} %constant.21.clone.lam_ref, f32[16]{0:T(128)} %constant.22.clone.lam_x_ref), custom_call_target="tpu_custom_call" | custom-call | tf_op jit(solution)/shard_map/pallas_call | solution.py:304
  24.4 16.3 %all_to_all.21.all_ref = f32[16,48,128]{2,1,0:T(8,128)} all-to-all(f32[16,48,128]{2,1,0:T(8,128)} %shard_map.110), channel_id=1, replica_groups=mesh['tm'=16,'space'=16] {'tm'}, dimensions={0} | all-to-all | bytes 786432 | tf_op jit(solution)/shard_map/all_to_all | solution.py:307
  40.7 2.7 %shard_map.111 = f32[16,256]{1,0:T(8,128)} custom-call(f32[768,128]{1,0:T(8,128)} %bitcast.6, f32[24,128]{1,0:T(8,128)} %constant.23.clone.lam_ref, f32[16]{0:T(128)} %constant.22.clone.lam_x_ref), custom_call_target="tpu_custom_call" | custom-call | tf_op jit(solution)/shard_map/pallas_call | solution.py:308
  43.4 1.6 %collective-permute-start.2 = (f32[16,256]{1,0:T(8,128)}, f32[16,256]{1,0:T(8,128)S(1)}, u32[]{:S(2)}, u32[]{:S(2)}) collective-permute-start(f32[16,256]{1,0:T(8,128)} %shard_map.111), channel_id=1, source_target_pairs={{0,1},{1,0},{2,3},{3,2},{4,5},{5,4},{6,7},{7,6},{8,9},{9,8},{10,11... | collective-permute-start | bytes 49160 | tf_op jit(solution)/shard_map/ppermute | solution.py:311
  45.0 1.0 %collective-permute-done.2 = f32[16,256]{1,0:T(8,128)S(1)} collective-permute-done((f32[16,256]{1,0:T(8,128)}, f32[16,256]{1,0:T(8,128)S(1)}, u32[]{:S(2)}, u32[]{:S(2)}) %collective-permute-start.2) | collective-permute-done | bytes 16416 | tf_op jit(solution)/shard_map/ppermute | solution.py:311
  46.0 0.7 add.3
  46.8 0.7 broadcast_in_dim.4
  47.4 3.4 %all-to-all-start.2 = ((f32[8,16,256]{2,1,0:T(8,128)}), f32[8,16,256]{2,1,0:T(8,128)S(1)}, u32[]{:S(2)}, u32[]{:S(2)}) async-start(f32[8,16,256]{2,1,0:T(8,128)} %broadcast_in_dim.4), calls=%async_computation.2 | async-start | bytes 262144 | tf_op jit(solution)/shard_map/all_to_all | solution.py:313
  50.8 0.0 copy-done
  50.9 2.3 %collective-permute-start.1 = (f32[3,2,64,128]{3,2,1,0:T(8,128)S(1)}, f32[3,2,64,128]{3,2,1,0:T(8,128)S(1)}, u32[]{:S(2)}, u32[]{:S(2)}) collective-permute-start(f32[3,2,64,128]{3,2,1,0:T(8,128)S(1)} %get-tuple-element.9), channel_id=1, source_target_pairs={{1,0},{2,1},{3,2},{4,3},{5,4},{6,5},{7,6},{8,7},{9,8},{10,9},{11,1... | collective-permute-start | bytes 589832 | tf_op jit(solution)/shard_map/ppermute | solution.py:295
  53.1 3.4 %collective-permute-start = (f32[3,2,64,128]{3,2,1,0:T(8,128)S(1)}, f32[3,2,64,128]{3,2,1,0:T(8,128)S(1)}, u32[]{:S(2)}, u32[]{:S(2)}) collective-permute-start(f32[3,2,64,128]{3,2,1,0:T(8,128)S(1)} %get-tuple-element.10), channel_id=1, source_target_pairs={{0,1},{1,2},{2,3},{3,4},{4,5},{5,6},{6,7},{7,8},{8,9},{9,10},{10,1... | collective-permute-start | bytes 589832 | tf_op jit(solution)/shard_map/ppermute | solution.py:294
  56.6 2.6 %all-to-all-done.2.sums_ref = f32[8,16,256]{2,1,0:T(8,128)S(1)} async-done(((f32[8,16,256]{2,1,0:T(8,128)}), f32[8,16,256]{2,1,0:T(8,128)S(1)}, u32[]{:S(2)}, u32[]{:S(2)}) %all-to-all-start.2) | async-done | bytes 131104 | tf_op jit(solution)/shard_map/all_to_all | solution.py:313
  59.2 0.7 copy-done.1
  59.8 5.1 %shard_map.112 = f32[128,128]{1,0:T(8,128)} custom-call(f32[8,16,256]{2,1,0:T(8,128)} %copy-done.1, f32[16,48,128]{2,1,0:T(8,128)} %all_to_all.21.all_ref, f32[128,32]{1,0:T(8,128)} %constant.24.clone.inv_z_ref, f32[24,128]{1,0:T(8,128)} %constant.23.clone.lam_ref, f32[16]{0:T(128)} %constant.22.clone.lam_x_ref), custom_call_target="tpu_custom_call" | custom-call | tf_op jit(solution)/shard_map/pallas_call | solution.py:321
  64.9 4.9 %all-to-all-start.3 = ((f32[16,8,128]{2,1,0:T(8,128)}), f32[16,8,128]{2,1,0:T(8,128)S(1)}, u32[]{:S(2)}, u32[]{:S(2)}) async-start(f32[16,8,128]{2,1,0:T(8,128)} %bitcast.10), calls=%async_computation.3 | async-start | bytes 131072 | tf_op jit(solution)/shard_map/all_to_all | solution.py:324
  69.8 0.0 collective-permute-done.1.above_ref
  69.8 0.0 collective-permute-done.below_ref
  69.8 0.0 copy-start.4
  69.8 7.8 %all-to-all-done.3.modes_ref = f32[16,8,128]{2,1,0:T(8,128)S(1)} async-done(((f32[16,8,128]{2,1,0:T(8,128)}), f32[16,8,128]{2,1,0:T(8,128)S(1)}, u32[]{:S(2)}, u32[]{:S(2)}) %all-to-all-start.3) | async-done | bytes 65568 | tf_op jit(solution)/shard_map/all_to_all | solution.py:324
  77.6 0.0 copy-done.4
  77.6 0.6 copy-done.2
  78.2 3.0 %shard_map.113 = f32[3,8,64,128]{3,2,1,0:T(8,128)} custom-call(f32[3,8,64,128]{3,2,1,0:T(8,128)} %get-tuple-element.7.fine_ref, f32[3,2,64,128]{3,2,1,0:T(8,128)} %copy-done.4, f32[3,2,64,128]{3,2,1,0:T(8,128)} %copy-done.3, f32[16,8,128]{2,1,0:T(8,128)} %copy-done.2, f32[64,16]{1,0:T(8,128)} %constant.25.clone.inv_x_ref, f32[128,384]{1,0:T(8,128)} %constant.26.clone.inv_y_ref), custom_call_target="tpu_custom_call" | custom-call | tf_op jit(solution)/shard_map/pallas_call | solution.py:325
  (6 shorter events, 0.0 us)
Async XLA Ops:
  4.5 46.3 %copy-start = (f32[1,3,8,64,128]{4,3,2,1,0:T(8,128)S(1)}, f32[1,3,8,64,128]{4,3,2,1,0:T(8,128)}, u32[]{:S(2)}) copy-start(f32[1,3,8,64,128]{4,3,2,1,0:T(8,128)} %param.11) | copy-start | bytes 2359300
  43.4 2.6 %collective-permute-start.2 = (f32[16,256]{1,0:T(8,128)}, f32[16,256]{1,0:T(8,128)S(1)}, u32[]{:S(2)}, u32[]{:S(2)}) collective-permute-start(f32[16,256]{1,0:T(8,128)} %shard_map.111), channel_id=1, source_target_pairs={{0,1},{1,0},{2,3},{3,2},{4,5},{5,4},{6,7},{7,6},{8,9},{9,8},{10,11... | collective-permute-start | bytes 49160 | tf_op jit(solution)/shard_map/ppermute | solution.py:311
  47.4 11.7 %all-to-all-start.2 = ((f32[8,16,256]{2,1,0:T(8,128)}), f32[8,16,256]{2,1,0:T(8,128)S(1)}, u32[]{:S(2)}, u32[]{:S(2)}) async-start(f32[8,16,256]{2,1,0:T(8,128)} %broadcast_in_dim.4), calls=%async_computation.2 | async-start | bytes 262144 | tf_op jit(solution)/shard_map/all_to_all | solution.py:313
  50.9 18.9 %collective-permute-start.1 = (f32[3,2,64,128]{3,2,1,0:T(8,128)S(1)}, f32[3,2,64,128]{3,2,1,0:T(8,128)S(1)}, u32[]{:S(2)}, u32[]{:S(2)}) collective-permute-start(f32[3,2,64,128]{3,2,1,0:T(8,128)S(1)} %get-tuple-element.9), channel_id=1, source_target_pairs={{1,0},{2,1},{3,2},{4,3},{5,4},{6,5},{7,6},{8,7},{9,8},{10,9},{11,1... | collective-permute-start | bytes 589832 | tf_op jit(solution)/shard_map/ppermute | solution.py:295
  53.1 16.7 %collective-permute-start = (f32[3,2,64,128]{3,2,1,0:T(8,128)S(1)}, f32[3,2,64,128]{3,2,1,0:T(8,128)S(1)}, u32[]{:S(2)}, u32[]{:S(2)}) collective-permute-start(f32[3,2,64,128]{3,2,1,0:T(8,128)S(1)} %get-tuple-element.10), channel_id=1, source_target_pairs={{0,1},{1,2},{2,3},{3,4},{4,5},{5,6},{6,7},{7,8},{8,9},{9,10},{10,1... | collective-permute-start | bytes 589832 | tf_op jit(solution)/shard_map/ppermute | solution.py:294
  59.2 0.7 copy-start.1
  64.9 12.7 %all-to-all-start.3 = ((f32[16,8,128]{2,1,0:T(8,128)}), f32[16,8,128]{2,1,0:T(8,128)S(1)}, u32[]{:S(2)}, u32[]{:S(2)}) async-start(f32[16,8,128]{2,1,0:T(8,128)} %bitcast.10), calls=%async_computation.3 | async-start | bytes 131072 | tf_op jit(solution)/shard_map/all_to_all | solution.py:324
  69.8 7.8 %copy-start.3 = (f32[3,2,64,128]{3,2,1,0:T(8,128)}, f32[3,2,64,128]{3,2,1,0:T(8,128)S(1)}, u32[]{:S(2)}) copy-start(f32[3,2,64,128]{3,2,1,0:T(8,128)S(1)} %collective-permute-done.1.above_ref) | copy-start | bytes 589828
  69.8 7.8 %copy-start.4 = (f32[3,2,64,128]{3,2,1,0:T(8,128)}, f32[3,2,64,128]{3,2,1,0:T(8,128)S(1)}, u32[]{:S(2)}) copy-start(f32[3,2,64,128]{3,2,1,0:T(8,128)S(1)} %collective-permute-done.below_ref) | copy-start | bytes 589828
  77.6 0.6 copy-start.2

commit v2 on v1

--- a/solution.py
+++ b/solution.py
@@ -79,7 +79,7 @@
         inv_z=f(inv_z.reshape(DEVICES_Z * 8, NZ)),
         lam=f(packed),
         lam_full=f(np.tile(full, (1, 4))),
-        lam_x=f(coarse_rate * ex),
+        lam_x=f(np.tile(coarse_rate * ex[:, None], (1, 128))),
     )
 
 
@@ -93,14 +93,63 @@
     return lax.broadcasted_iota(jnp.int32, shape, dim)
 
 
-def fine_kernel(field_ref, strain_ref, fwd_x_ref, fwd_y_ref, fine_ref, coarse_ref, sums):
-    sums[...] = jnp.zeros_like(sums)
+def around(f, width):
+    total = pltpu.roll(f, width, 0) + pltpu.roll(f, CX - width, 0)
+    return total + pltpu.roll(f, width, 1) + pltpu.roll(f, CY - width, 1)
+
+
+def coarse_kernel(field_ref, strain_ref, fwd_x_ref, fwd_y_ref, coarse_ref, sums):
+    near = diffusion * kernel_near
+    far = diffusion * kernel_far
+
+    def block(q, _):
+        basis = [None] * 3
+        stretch = [None] * 3
+        for k in range(COARSEN):
+            z = COARSEN * q + k
+            comps = [field_ref[c, z] for c in range(3)]
+            for c in range(3):
+                acc = strain_ref[3 * c, z].astype(jnp.float32) * comps[0]
+                for j in range(1, 3):
+                    acc = acc + strain_ref[3 * c + j, z].astype(jnp.float32) * comps[j]
+                stretch[c] = acc if k == 0 else stretch[c] + acc
+                basis[c] = comps[c] if k == 0 else basis[c] + comps[c]
+        for c in range(3):
+            lanes = slice(c * CY, (c + 1) * CY)
+            total = basis[c]
+            sums[q, :, lanes] = total
+            sums[2 + q, :, lanes] = (
+                (1.0 - 4.0 * (near + far)) * total
+                + stretch[c]
+                + near * around(total, 1)
+                + far * around(total, 2)
+            )
+        return 0
+
+    lax.fori_loop(0, 2, block, 0)
+    for c in range(3):
+        lanes = slice(c * CY, (c + 1) * CY)
+        low = [diffusion * field_ref[c, 4 * q] + far * field_ref[c, 4 * q + 1] for q in range(2)]
+        high = [diffusion * field_ref[c, 4 * q + 3] + far * field_ref[c, 4 * q + 2] for q in range(2)]
+        middle = low[1] - high[0]
+        sums[2, :, lanes] += middle - low[0]
+        sums[3, :, lanes] -= middle + high[1]
+        sums[4, :, lanes] = low[0]
+        sums[5, :, lanes] = high[1]
+    along_x = [dot(fwd_x_ref[...], sums[q]) for q in range(6)]
+    modes = dot(jnp.concatenate(along_x, axis=0), fwd_y_ref[...])
+    for q in range(6):
+        coarse_ref[:, q, :] = modes[NX * q : NX * (q + 1)]
+    for q in range(6, 8):
+        coarse_ref[:, q, :] = jnp.zeros((NX, 128), jnp.float32)
+
+
+def fine_kernel(field_ref, strain_ref, below_ref, above_ref, fine_ref):
     near = diffusion * kernel_near
     far = diffusion * kernel_far
     centre = 1.0 - 6.0 * (near + far)
 
     def plane(z, _):
-        block = z // COARSEN
         up1, up2 = jnp.minimum(z + 1, DEPTH - 1), jnp.minimum(z + 2, DEPTH - 1)
         dn1, dn2 = jnp.maximum(z - 1, 0), jnp.maximum(z - 2, 0)
         w_up1 = jnp.where(z + 1 < DEPTH, near, 0.0).astype(jnp.float32)
@@ -110,36 +159,24 @@
         comps = [field_ref[c, z] for c in range(3)]
         for c in range(3):
             f = comps[c]
-            near_sum = pltpu.roll(f, 1, 0) + pltpu.roll(f, CX - 1, 0)
-            near_sum = near_sum + pltpu.roll(f, 1, 1) + pltpu.roll(f, CY - 1, 1)
-            far_sum = pltpu.roll(f, 2, 0) + pltpu.roll(f, CX - 2, 0)
-            far_sum = far_sum + pltpu.roll(f, 2, 1) + pltpu.roll(f, CY - 2, 1)
-            acc = centre * f + near * near_sum + far * far_sum
+            acc = centre * f + near * around(f, 1) + far * around(f, 2)
             acc = acc + w_up1 * field_ref[c, up1] + w_dn1 * field_ref[c, dn1]
             acc = acc + w_up2 * field_ref[c, up2] + w_dn2 * field_ref[c, dn2]
             for j in range(3):
                 acc = acc + strain_ref[3 * c + j, z].astype(jnp.float32) * comps[j]
             fine_ref[c, z] = acc
-            lanes = slice(c * CY, (c + 1) * CY)
-            sums[block, :, lanes] += f
-            sums[2 + block, :, lanes] += acc
         return 0
 
     lax.fori_loop(0, DEPTH, plane, 0)
     for c in range(3):
-        lanes = slice(c * CY, (c + 1) * CY)
-        sums[4, :, lanes] = diffusion * field_ref[c, 0] + far * field_ref[c, 1]
-        sums[5, :, lanes] = diffusion * field_ref[c, DEPTH - 1] + far * field_ref[c, DEPTH - 2]
-    along_x = [dot(fwd_x_ref[...], sums[q]) for q in range(6)]
-    modes = dot(jnp.concatenate(along_x, axis=0), fwd_y_ref[...])
-    for q in range(6):
-        coarse_ref[:, q, :] = modes[NX * q : NX * (q + 1)]
-    for q in range(6, 8):
-        coarse_ref[:, q, :] = jnp.zeros((NX, 128), jnp.float32)
+        fine_ref[c, 0] += near * below_ref[c, 1] + far * below_ref[c, 0]
+        fine_ref[c, 1] += far * below_ref[c, 1]
+        fine_ref[c, DEPTH - 2] += far * above_ref[c, 0]
+        fine_ref[c, DEPTH - 1] += near * above_ref[c, 0] + far * above_ref[c, 1]
 
 
 def depth_kernel(modes_ref, fwd_z_ref, lam_ref, lam_x_ref, out_ref):
-    lam = lam_ref[...] + lam_x_ref[lax.axis_index("space")]
+    lam = lam_ref[...] + lam_x_ref[pl.ds(lax.axis_index("space"), 1), :]
     both = dot(fwd_z_ref[...], modes_ref[...])
     basis = both[:NZ]
     defect = both[NZ:] - lam * basis
@@ -156,7 +193,7 @@
 
 
 def gram_kernel(all_ref, lam_ref, lam_x_ref, out_ref):
-    shift = lam_x_ref[lax.axis_index("space")]
+    shift = lam_x_ref[pl.ds(lax.axis_index("space"), 1), :]
     sub = iota((8, 128), 0)
     total = jnp.zeros((64, 88), jnp.float32)
     for r in range(0, ROWS, 2):
@@ -193,7 +230,7 @@
 
 
 def solve_kernel(sums_ref, all_ref, inv_z_ref, lam_ref, lam_x_ref, out_ref):
-    shift = lam_x_ref[lax.axis_index("space")]
+    shift = lam_x_ref[pl.ds(lax.axis_index("space"), 1), :]
     slice_index = lax.axis_index("tm")
     parts = sums_ref.shape[0]
     total = sums_ref[0]
@@ -202,33 +239,55 @@
     low, high = total[:, :128], total[:, 128:]
     lane = iota((16, 128), 1)
     sub = iota((16, 128), 0)
+    columns = [jnp.broadcast_to(high[:, 96 + i : 97 + i], (16, 128)) for i in range(SLICES)]
     for i in range(SLICES):
-        column = high[:, 96 + i : 97 + i]
-        scale = 1.0 / column[i : i + 1]
-        factor = jnp.where(sub[:, :1] == i, column - 1.0, column) * scale
+        column = columns[i]
+        factor = jnp.where(sub == i, column - 1.0, column) * (1.0 / column[i : i + 1])
+        for j in range(i + 1, SLICES):
+            columns[j] = columns[j] - factor * columns[j][i : i + 1]
         low, high = low - factor * low[i : i + 1], high - factor * high[i : i + 1]
+
+    def shifted(pair, by):
+        rolled = [pltpu.roll(v, 128 - by, 1) for v in pair]
+        inside = lane < 128 - by
+        return jnp.where(inside, rolled[0], rolled[1]), jnp.where(inside, rolled[1], 0.0)
+
     diag = (lane & 15) == sub
     spread = (lane >> 3) == sub
     block = (iota((8, 128), 1) & 7) == iota((8, 128), 0)
-    h_high = jnp.where(lane < 96, high, 0.0)
-    acc_low = jnp.zeros((16, 128), jnp.float32)
-    acc_high = jnp.zeros((16, 128), jnp.float32)
+    starts = [high, None]
+    one = (low, jnp.where(lane < 96, high, 0.0))
+    one_next = shifted(one, 16)
+    twice = dot(low[:, :16], jnp.concatenate([low, high], axis=1))
+    starts[1] = twice[:, 128:] + pltpu.roll(high, 127, 1)
+    two = (twice[:, :128] + one_next[0], jnp.where(lane < 80, twice[:, 128:] + one_next[1], 0.0))
+    two_next = shifted(two, 16)
+    acc_one = acc_two = None
     first = jnp.where(iota((1, 128), 1) < 8, 1.0, 0.0)
     weights = [jnp.where(block, first, 0.0)]
-    for k in range(1, SLICES):
-        at = jnp.where(lane < 16, acc_low, 0.0) + jnp.where(lane == 112 + k - 1, high, 0.0)
-        c = jnp.sum(at, axis=1, keepdims=True)
-        weights.append(
-            jnp.where(block, jnp.sum(jnp.where(spread, c, 0.0), axis=0, keepdims=True), 0.0)
-        )
-        if k < SLICES - 1:
-            row = jnp.sum(jnp.where(diag, c, 0.0), axis=0, keepdims=True)
-            shifted_low, shifted_high = pltpu.roll(acc_low, 112, 1), pltpu.roll(acc_high, 112, 1)
-            if k > 1:
-                acc_low = jnp.where(lane < 112, shifted_low, shifted_high)
-                acc_high = jnp.where(lane < 112, shifted_high, 0.0)
-            acc_low = acc_low + low * row
-            acc_high = acc_high + h_high * row
+    for n in range(0, SLICES, 2):
+        found = []
+        for acc, start in ((acc_one, starts[0]), (acc_two, starts[1])):
+            if n == SLICES - 2 and found:
+                break
+            at = jnp.where(lane == 112 + n, start, 0.0)
+            if n > 0:
+                at = at + jnp.where(lane < 16, acc[0], 0.0)
+            c = jnp.sum(at, axis=1, keepdims=True)
+            found.append(c)
+            weights.append(
+                jnp.where(block, jnp.sum(jnp.where(spread, c, 0.0), axis=0, keepdims=True), 0.0)
+            )
+        if n < SLICES - 2:
+            older, newer = [
+                jnp.sum(jnp.where(diag, c, 0.0), axis=0, keepdims=True) for c in found
+            ]
+            grown_one = [a * newer + b * older for a, b in zip(one, one_next)]
+            grown_two = [a * newer + b * older for a, b in zip(two, two_next)]
+            if n > 0:
+                grown_one = [a + b for a, b in zip(grown_one, shifted(acc_one, 32))]
+                grown_two = [a + b for a, b in zip(grown_two, shifted(acc_two, 32))]
+            acc_one, acc_two = grown_one, grown_two
     weights = jnp.concatenate(weights, axis=0)
     tiles = []
     for g in range(3):
@@ -250,81 +309,101 @@
     out_ref[...] = dot(inv_z_ref[...], jnp.concatenate(tiles + [rest], axis=0))
 
 
-def finish_kernel(fine_ref, below_ref, above_ref, modes_ref, inv_x_ref, inv_y_ref, out_ref):
-    near = diffusion * kernel_near
-    far = diffusion * kernel_far
+def pair_kernel(mine_ref, other_ref, out_ref):
+    total = mine_ref[...] + other_ref[...]
+    for i in range(out_ref.shape[0]):
+        out_ref[i] = total
+
+
+def finish_kernel(fine_ref, modes_ref, inv_x_ref, inv_y_ref, out_hbm, out_ref, sem):
+    copies = []
     for q in range(2):
-        along_x = dot(inv_x_ref[...], modes_ref[:, q, :])
-        both = dot(along_x, inv_y_ref[...])
+        both = dot(dot(inv_x_ref[...], modes_ref[:, q, :]), inv_y_ref[...])
         for c in range(3):
             carried = both[:, c * CY : (c + 1) * CY]
             for k in range(COARSEN):
                 z = COARSEN * q + k
-                value = fine_ref[c, z] + carried
-                if z == 0:
-                    value = value + near * below_ref[c, 1] + far * below_ref[c, 0]
-                if z == 1:
-                    value = value + far * below_ref[c, 1]
-                if z == DEPTH - 1:
-                    value = value + near * above_ref[c, 0] + far * above_ref[c, 1]
-                if z == DEPTH - 2:
-                    value = value + far * above_ref[c, 0]
-                out_ref[c, z] = value
+                out_ref[c, z] = fine_ref[c, z] + carried
+            planes = pl.ds(COARSEN * q, COARSEN)
+            copy = pltpu.make_async_copy(
+                out_ref.at[c, planes], out_hbm.at[c, planes], sem.at[q, c]
+            )
+            copy.start()
+            copies.append(copy)
+    for copy in copies:
+        copy.wait()
 
 
 VMEM = pl.BlockSpec(memory_space=pltpu.VMEM)
 SMEM = pl.BlockSpec(memory_space=pltpu.SMEM)
-
-
-def call(kernel, shapes, specs, scratch=()):
-    out = jax.tree.map(lambda s: jax.ShapeDtypeStruct(s, jnp.float32), shapes, is_leaf=lambda s: isinstance(s, tuple) and isinstance(s[0], int))
+HBM = pl.BlockSpec(memory_space=pltpu.HBM)
+
+
+def fast(x):
+    return pltpu.with_memory_space_constraint(x, pltpu.VMEM)
+
+
+def call(kernel, outs, specs, scratch=(), out_specs=None):
     return pl.pallas_call(
         kernel,
-        out_shape=out,
+        out_shape=outs,
         in_specs=specs,
-        out_specs=jax.tree.map(lambda _: VMEM, out),
+        out_specs=VMEM if out_specs is None else out_specs,
         scratch_shapes=list(scratch),
     )
 
 
+def near_array(*shape):
+    return pltpu.VMEM(shape, jnp.float32)
+
+
+def far_array(*shape):
+    return jax.ShapeDtypeStruct(shape, jnp.float32)
+
+
 def local(starts, strain):
-    con = constants()
+    first = ("fwd_x", "wide_fwd_y")
+    con = {k: v if k in first else fast(jnp.asarray(v)) for k, v in constants().items()}
     field, rates = starts[0], strain[0]
     count = lax.axis_size("space")
-    below = lax.ppermute(field[:, DEPTH - 2 :], "space", [(i, i + 1) for i in range(count - 1)])
-    above = lax.ppermute(field[:, :2], "space", [(i + 1, i) for i in range(count - 1)])
-
-    fine, coarse = call(
-        fine_kernel,
-        [(3, DEPTH, CX, CY), (NX, 8, 128)],
+
+    coarse = call(
+        coarse_kernel,
+        near_array(NX, 8, 128),
         [VMEM] * 4,
         [pltpu.VMEM((6, CX, 3 * CY), jnp.float32)],
     )(field, rates, con["fwd_x"], con["wide_fwd_y"])
     coarse = lax.all_to_all(coarse, "space", 0, 0, tiled=True)
-    mine = call(depth_kernel, (SLICES, 2 * ROWS, 128), [VMEM] * 3 + [SMEM])(
-        coarse.reshape(128, 128), con["fwd_z"], con["lam_full"], con["lam_x"]
-    )
+    mine = call(depth_kernel, near_array(SLICES, 2 * ROWS, 128), [VMEM] * 4)(
+        fast(coarse.reshape(128, 128)), con["fwd_z"], con["lam_full"], con["lam_x"]
+    )
+    later, mine = lax.optimization_barrier((field, mine))
     every = lax.all_to_all(mine, "tm", 0, 0, tiled=True)
-    share = call(gram_kernel, (SLICES, 256), [VMEM] * 2 + [SMEM])(
-        every.reshape(SLICES * 2 * ROWS, 128), con["lam"], con["lam_x"]
-    )
-    share = share + lax.ppermute(share, "space", [(i, i ^ 1) for i in range(count)])
+    below = lax.ppermute(later[:, DEPTH - 2 :], "space", [(i, i + 1) for i in range(count - 1)])
+    above = lax.ppermute(later[:, :2], "space", [(i + 1, i) for i in range(count - 1)])
+    share = call(gram_kernel, near_array(SLICES, 256), [VMEM] * 3)(
+        fast(every.reshape(SLICES * 2 * ROWS, 128)), con["lam"], con["lam_x"]
+    )
+    fine = call(fine_kernel, near_array(*field.shape), [VMEM] * 4)(
+        later, rates, fast(below), fast(above)
+    )
+    other = lax.ppermute(share, "space", [(i, i ^ 1) for i in range(count)])
+    pair = call(pair_kernel, near_array(count // 2, *share.shape), [VMEM] * 2)(
+        fast(share), fast(other)
+    )
     groups = [list(range(0, count, 2)), list(range(1, count, 2))]
-    shares = lax.all_to_all(
-        jnp.broadcast_to(share[None], (count // 2,) + share.shape),
-        "space",
-        0,
-        0,
-        axis_index_groups=groups,
-        tiled=True,
-    )
-    carried = call(solve_kernel, (128, 128), [VMEM] * 4 + [SMEM])(
-        shares, every, con["inv_z"], con["lam"], con["lam_x"]
+    shares = lax.all_to_all(pair, "space", 0, 0, axis_index_groups=groups, tiled=True)
+    carried = call(solve_kernel, near_array(128, 128), [VMEM] * 5)(
+        fast(shares), fast(every), con["inv_z"], con["lam"], con["lam_x"]
     )
     carried = lax.all_to_all(carried.reshape(DEVICES_Z, 8, 128), "space", 0, 0, tiled=True)
-    corrected = call(finish_kernel, (3, DEPTH, CX, CY), [VMEM] * 6)(
-        fine, below, above, carried, con["inv_x"], con["wide_inv_y"]
-    )
+    corrected = call(
+        finish_kernel,
+        far_array(*field.shape),
+        [VMEM] * 4,
+        [pltpu.VMEM(field.shape, jnp.float32), pltpu.SemaphoreType.DMA((2, 3))],
+        HBM,
+    )(fast(fine), fast(carried), con["inv_x"], con["wide_inv_y"])
     return corrected[None]
 
 

time: 81.8 us -> 70.2 us (0.86)
  Pallas kernels: 17.1 us -> 12 us
  waiting for transfers between devices: 11.5 us -> 8.08 us
  local copies, waits for them, and re-layouts: 1.97 us -> 0.07 us
    pallas_call x5 -> x7, Pallas kernels: 17.1 us -> 12 us  [the longest x1 3.14 us: local(): call(fine_kernel, near_array(*field.shape), [VMEM] * 4)]
    all_to_all x1, waiting for transfers between devices: 7.8 us -> 4.64 us  [local(): lax.all_to_all(carried.reshape(DEVICES_Z, 8, 128), 'space', 0, 0, tiled=T...]
    unnamed x10 -> x16, local copies, waits for them, and re-layouts: 1.28 us -> 0.04 us
  transfers between devices with their start and end apart: 5 -> 5, of which waited for: 3 -> 3; matrix products, arithmetic and copies ran while one was open for 0% -> 0% of each run, Pallas kernels for 6% -> 8%
where the time goes in v2:
time: 70.2 us; the launch traced here: 69.7 us
  blocking collectives  33.9 us (48%)
  starting transfers between devices  15.6 us (22%)
  Pallas kernels  12 us (17%)
  waiting for transfers between devices  8.08 us (12%)
    all_to_all x1, blocking collectives, local(): coarse = lax.all_to_all(coarse, 'space', 0, 0, tiled=True)  17.7 us
    all_to_all x1, blocking collectives, local(): every = lax.all_to_all(mine, 'tm', 0, 0, tiled=True)  16.2 us
    all_to_all x1, starting transfers between devices, local(): lax.all_to_all(carried.reshape(DEVICES_Z, 8, 128), 'space', 0, 0, tiled=T...  4.87 us
    all_to_all x1, waiting for transfers between devices, local(): lax.all_to_all(carried.reshape(DEVICES_Z, 8, 128), 'space', 0, 0, tiled=T...  4.64 us
    ppermute x1, starting transfers between devices, local(): lax.ppermute(later[:, DEPTH - 2:], 'space', [(i, i + 1) for i in range(co...  3.43 us
    all_to_all x1, starting transfers between devices, local(): lax.all_to_all(pair, 'space', 0, 0, axis_index_groups=groups, tiled=True)  3.37 us
    pallas_call x1, Pallas kernels, local(): call(fine_kernel, near_array(*field.shape), [VMEM] * 4)  3.14 us
    pallas_call x1, Pallas kernels, local(): call(coarse_kernel, near_array(NX, 8, 128), [VMEM] * 4, [pltpu.VMEM((6, C...  2.7 us
  transfers between devices with their start and end apart: 5, of which 3 were waited for; matrix products, arithmetic and copies ran while one was open for 0% of the time, Pallas kernels for 8%

profile of v2, /device:TPU:1, one launch (start us, length us, event | category | flops | bytes accessed | tf_op | source)
XLA Modules:
  0.0 69.7 jit_solution(12810163534811507953)
XLA Ops:
  0.0 2.7 %shard_map.109 = f32[16,8,128]{2,1,0:T(8,128)S(1)} custom-call(f32[3,8,64,128]{3,2,1,0:T(8,128)} %bitcast.8, bf16[9,8,64,128]{3,2,1,0:T(8,128)(2,1)} %bitcast.11, f32[16,64]{1,0:T(8,128)} %constant.25.clone.fwd_x_ref, f32[384,128]{1,0:T(8,128)} %constant.26.clone.fwd_y_ref), custom_call_target="tpu_custom_call" | custom-call | tf_op jit(solution)/shard_map/pallas_call | solution.py:370
  2.7 0.0 copy-start.3
  2.7 0.0 copy-start.7
  2.7 17.7 %all_to_all.20 = f32[16,8,128]{2,1,0:T(8,128)S(1)} all-to-all(f32[16,8,128]{2,1,0:T(8,128)S(1)} %shard_map.109), channel_id=1, replica_groups=mesh['tm'=16,'space'=16] {'space'}, dimensions={0} | all-to-all | bytes 131072 | tf_op jit(solution)/shard_map/all_to_all | solution.py:376
  20.5 0.0 copy-done.5
  20.5 0.3 shard_map.110
  20.7 0.0 copy-start.2
  20.8 16.2 %all_to_all.21.all_ref = f32[16,48,128]{2,1,0:T(8,128)S(1)} all-to-all(f32[16,48,128]{2,1,0:T(8,128)S(1)} %shard_map.110), channel_id=1, replica_groups=mesh['tm'=16,'space'=16] {'tm'}, dimensions={0} | all-to-all | bytes 786432 | tf_op jit(solution)/shard_map/all_to_all | solution.py:381
  36.9 1.2 %shard_map.112.mine_ref = f32[16,256]{1,0:T(8,128)S(1)} custom-call(f32[768,128]{1,0:T(8,128)S(1)} %bitcast.6, f32[24,128]{1,0:T(8,128)S(1)} %copy-done.3, f32[16,128]{1,0:T(8,128)S(1)} %copy-done.1), custom_call_target="tpu_custom_call" | custom-call | tf_op jit(solution)/shard_map/pallas_call | solution.py:384
  38.1 1.7 %collective-permute-start.2 = (f32[16,256]{1,0:T(8,128)S(1)}, f32[16,256]{1,0:T(8,128)S(1)}, u32[]{:S(2)}, u32[]{:S(2)}) collective-permute-start(f32[16,256]{1,0:T(8,128)S(1)} %shard_map.112.mine_ref), channel_id=1, source_target_pairs={{0,1},{1,0},{2,3},{3,2},{4,5},{5,4},{6,7},{7,6},{8,9},{9,8},{10,11... | collective-permute-start | bytes 49160 | tf_op jit(solution)/shard_map/ppermute | solution.py:390
  39.7 0.8 %collective-permute-done.2.other_ref = f32[16,256]{1,0:T(8,128)S(1)} collective-permute-done((f32[16,256]{1,0:T(8,128)S(1)}, f32[16,256]{1,0:T(8,128)S(1)}, u32[]{:S(2)}, u32[]{:S(2)}) %collective-permute-start.2) | collective-permute-done | bytes 16416 | tf_op jit(solution)/shard_map/ppermute | solution.py:390
  40.6 0.7 shard_map.113
  41.3 3.4 %all-to-all-start.2 = ((f32[8,16,256]{2,1,0:T(8,128)}), f32[8,16,256]{2,1,0:T(8,128)S(1)}, u32[]{:S(2)}, u32[]{:S(2)}) async-start(f32[8,16,256]{2,1,0:T(8,128)} %shard_map.113), calls=%async_computation.2 | async-start | bytes 262144 | tf_op jit(solution)/shard_map/all_to_all | solution.py:395
  44.7 2.3 %collective-permute-start.1 = (f32[3,2,64,128]{3,2,1,0:T(8,128)S(1)}, f32[3,2,64,128]{3,2,1,0:T(8,128)S(1)}, u32[]{:S(2)}, u32[]{:S(2)}) collective-permute-start(f32[3,2,64,128]{3,2,1,0:T(8,128)S(1)} %get-tuple-element.9), channel_id=1, source_target_pairs={{1,0},{2,1},{3,2},{4,3},{5,4},{6,5},{7,6},{8,7},{9,8},{10,9},{11,1... | collective-permute-start | bytes 589832 | tf_op jit(solution)/shard_map/ppermute | solution.py:383
  46.9 3.4 %collective-permute-start = (f32[3,2,64,128]{3,2,1,0:T(8,128)S(1)}, f32[3,2,64,128]{3,2,1,0:T(8,128)S(1)}, u32[]{:S(2)}, u32[]{:S(2)}) collective-permute-start(f32[3,2,64,128]{3,2,1,0:T(8,128)S(1)} %get-tuple-element.10), channel_id=1, source_target_pairs={{0,1},{1,2},{2,3},{3,4},{4,5},{5,6},{6,7},{7,8},{8,9},{9,10},{10,1... | collective-permute-start | bytes 589832 | tf_op jit(solution)/shard_map/ppermute | solution.py:382
  50.4 2.6 %all-to-all-done.2.sums_ref = f32[8,16,256]{2,1,0:T(8,128)S(1)} async-done(((f32[8,16,256]{2,1,0:T(8,128)}), f32[8,16,256]{2,1,0:T(8,128)S(1)}, u32[]{:S(2)}, u32[]{:S(2)}) %all-to-all-start.2) | async-done | bytes 131104 | tf_op jit(solution)/shard_map/all_to_all | solution.py:395
  53.0 2.6 %shard_map.114 = f32[128,128]{1,0:T(8,128)} custom-call(f32[8,16,256]{2,1,0:T(8,128)S(1)} %all-to-all-done.2.sums_ref, f32[16,48,128]{2,1,0:T(8,128)S(1)} %all_to_all.21.all_ref, f32[128,32]{1,0:T(8,128)S(1)} %copy-done.2, f32[24,128]{1,0:T(8,128)S(1)} %copy-done.3, f32[16,128]{1,0:T(8,128)S(1)} %copy-done.1), custom_call_target="tpu_custom_call" | custom-call | tf_op jit(solution)/shard_map/pallas_call | solution.py:396
  55.5 4.9 %all-to-all-start.3 = ((f32[16,8,128]{2,1,0:T(8,128)}), f32[16,8,128]{2,1,0:T(8,128)S(1)}, u32[]{:S(2)}, u32[]{:S(2)}) async-start(f32[16,8,128]{2,1,0:T(8,128)} %bitcast.4), calls=%async_computation.3 | async-start | bytes 131072 | tf_op jit(solution)/shard_map/all_to_all | solution.py:399
  60.4 0.0 copy-start.4
  60.4 0.0 collective-permute-done.1.above_ref
  60.5 0.0 collective-permute-done.below_ref
  60.5 3.1 %shard_map.111.fine_ref = f32[3,8,64,128]{3,2,1,0:T(8,128)S(1)} custom-call(f32[3,8,64,128]{3,2,1,0:T(8,128)} %bitcast.9, bf16[9,8,64,128]{3,2,1,0:T(8,128)(2,1)} %bitcast.12, f32[3,2,64,128]{3,2,1,0:T(8,128)S(1)} %collective-permute-done.below_ref, f32[3,2,64,128]{3,2,1,0:T(8,128)S(1)} %collective-permute-done.1.above_ref), custom_call_target="tpu_custom_call" | custom-call | tf_op jit(solution)/shard_map/pallas_call | solution.py:387
  63.6 4.6 %all-to-all-done.3.modes_ref = f32[16,8,128]{2,1,0:T(8,128)S(1)} async-done(((f32[16,8,128]{2,1,0:T(8,128)}), f32[16,8,128]{2,1,0:T(8,128)S(1)}, u32[]{:S(2)}, u32[]{:S(2)}) %all-to-all-start.3) | async-done | bytes 65568 | tf_op jit(solution)/shard_map/all_to_all | solution.py:399
  68.3 1.5 %shard_map.115 = f32[3,8,64,128]{3,2,1,0:T(8,128)} custom-call(f32[3,8,64,128]{3,2,1,0:T(8,128)S(1)} %shard_map.111.fine_ref, f32[16,8,128]{2,1,0:T(8,128)S(1)} %all-to-all-done.3.modes_ref, f32[64,16]{1,0:T(8,128)S(1)} %copy-done.4, f32[128,384]{1,0:T(8,128)S(1)} %copy-done), custom_call_target="tpu_custom_call" | custom-call | tf_op jit(solution)/shard_map/pallas_call | solution.py:400
  (12 shorter events, 0.0 us)
Async XLA Ops:
  0.0 20.5 %copy-start.1 = (f32[16,128]{1,0:T(8,128)S(1)}, f32[16,128]{1,0:T(8,128)}, u32[]{:S(2)}) copy-start(f32[16,128]{1,0:T(8,128)} %constant.24.clone.lam_x_ref) | copy-start | bytes 24580
  0.0 20.5 %copy-start.5 = (f32[64,128]{1,0:T(8,128)S(1)}, f32[64,128]{1,0:T(8,128)}, u32[]{:S(2)}) copy-start(f32[64,128]{1,0:T(8,128)} %constant.20.clone.fwd_z_ref) | copy-start | bytes 98308
  0.0 20.5 %copy-start.6 = (f32[32,128]{1,0:T(8,128)S(1)}, f32[32,128]{1,0:T(8,128)}, u32[]{:S(2)}) copy-start(f32[32,128]{1,0:T(8,128)} %constant.23.clone.lam_ref) | copy-start | bytes 49156
  2.7 34.2 %copy-start.3 = (f32[24,128]{1,0:T(8,128)S(1)}, f32[24,128]{1,0:T(8,128)}, u32[]{:S(2)}) copy-start(f32[24,128]{1,0:T(8,128)} %constant.22.clone.lam_ref) | copy-start | bytes 36868
  2.7 41.9 %copy-start.7 = (f32[1,3,8,64,128]{4,3,2,1,0:T(8,128)S(1)}, f32[1,3,8,64,128]{4,3,2,1,0:T(8,128)}, u32[]{:S(2)}) copy-start(f32[1,3,8,64,128]{4,3,2,1,0:T(8,128)} %param.11) | copy-start | bytes 2359300
  20.7 32.2 %copy-start.2 = (f32[128,32]{1,0:T(8,128)S(1)}, f32[128,32]{1,0:T(8,128)}, u32[]{:S(2)}) copy-start(f32[128,32]{1,0:T(8,128)} %constant.21.clone.inv_z_ref) | copy-start | bytes 49156
  38.1 2.5 %collective-permute-start.2 = (f32[16,256]{1,0:T(8,128)S(1)}, f32[16,256]{1,0:T(8,128)S(1)}, u32[]{:S(2)}, u32[]{:S(2)}) collective-permute-start(f32[16,256]{1,0:T(8,128)S(1)} %shard_map.112.mine_ref), channel_id=1, source_target_pairs={{0,1},{1,0},{2,3},{3,2},{4,5},{5,4},{6,7},{7,6},{8,9},{9,8},{10,11... | collective-permute-start | bytes 49160 | tf_op jit(solution)/shard_map/ppermute | solution.py:390
  41.3 11.7 %all-to-all-start.2 = ((f32[8,16,256]{2,1,0:T(8,128)}), f32[8,16,256]{2,1,0:T(8,128)S(1)}, u32[]{:S(2)}, u32[]{:S(2)}) async-start(f32[8,16,256]{2,1,0:T(8,128)} %shard_map.113), calls=%async_computation.2 | async-start | bytes 262144 | tf_op jit(solution)/shard_map/all_to_all | solution.py:395
  44.7 15.8 %collective-permute-start.1 = (f32[3,2,64,128]{3,2,1,0:T(8,128)S(1)}, f32[3,2,64,128]{3,2,1,0:T(8,128)S(1)}, u32[]{:S(2)}, u32[]{:S(2)}) collective-permute-start(f32[3,2,64,128]{3,2,1,0:T(8,128)S(1)} %get-tuple-element.9), channel_id=1, source_target_pairs={{1,0},{2,1},{3,2},{4,3},{5,4},{6,5},{7,6},{8,7},{9,8},{10,9},{11,1... | collective-permute-start | bytes 589832 | tf_op jit(solution)/shard_map/ppermute | solution.py:383
  46.9 13.5 %collective-permute-start = (f32[3,2,64,128]{3,2,1,0:T(8,128)S(1)}, f32[3,2,64,128]{3,2,1,0:T(8,128)S(1)}, u32[]{:S(2)}, u32[]{:S(2)}) collective-permute-start(f32[3,2,64,128]{3,2,1,0:T(8,128)S(1)} %get-tuple-element.10), channel_id=1, source_target_pairs={{0,1},{1,2},{2,3},{3,4},{4,5},{5,6},{6,7},{7,8},{8,9},{9,10},{10,1... | collective-permute-start | bytes 589832 | tf_op jit(solution)/shard_map/ppermute | solution.py:382
  55.5 12.7 %all-to-all-start.3 = ((f32[16,8,128]{2,1,0:T(8,128)}), f32[16,8,128]{2,1,0:T(8,128)S(1)}, u32[]{:S(2)}, u32[]{:S(2)}) async-start(f32[16,8,128]{2,1,0:T(8,128)} %bitcast.4), calls=%async_computation.3 | async-start | bytes 131072 | tf_op jit(solution)/shard_map/all_to_all | solution.py:399
  60.4 7.8 %copy-start = (f32[128,384]{1,0:T(8,128)S(1)}, f32[128,384]{1,0:T(8,128)}, u32[]{:S(2)}) copy-start(f32[128,384]{1,0:T(8,128)} %constant.19.clone.inv_y_ref) | copy-start | bytes 589828
  60.4 7.8 %copy-start.4 = (f32[64,16]{1,0:T(8,128)S(1)}, f32[64,16]{1,0:T(8,128)}, u32[]{:S(2)}) copy-start(f32[64,16]{1,0:T(8,128)} %constant.18.clone.inv_x_ref) | copy-start | bytes 12292

commit v3 on v2

--- a/solution.py
+++ b/solution.py
@@ -44,7 +44,7 @@
     ez = 2 * np.cos(np.pi * k / (NZ + 1))
     spread_x = np.repeat(np.eye(NX), COARSEN, axis=0)
     spread_y = np.repeat(np.eye(NY), COARSEN, axis=0)
-    fwd_x = fx @ spread_x.T / 16.0
+    fwd_x = fx / 16.0
     fwd_y = spread_y @ fy.T / 4.0
     inv_x = spread_x @ fx.T
     inv_y = fy @ spread_y.T
@@ -54,12 +54,10 @@
         wide_fwd_y[c * CY : (c + 1) * CY, 32 * c : 32 * c + 32] = fwd_y
         wide_inv_y[32 * c : 32 * c + 32, c * CY : (c + 1) * CY] = inv_y
     fwd_z = np.zeros((2 * NZ, DEVICES_Z, 8))
-    inv_z = np.zeros((DEVICES_Z, 8, NZ))
     for s in range(DEVICES_Z):
         for q in range(2):
             fwd_z[:NZ, s, q] = sz[:, 2 * s + q]
             fwd_z[NZ:, s, 2 + q] = sz[:, 2 * s + q]
-            inv_z[s, q] = sz[2 * s + q]
         if s > 0:
             fwd_z[NZ:, s, 4] = sz[:, 2 * s - 1]
         if s < DEVICES_Z - 1:
@@ -76,7 +74,7 @@
         inv_x=f(inv_x),
         wide_inv_y=f(wide_inv_y),
         fwd_z=f(fwd_z.reshape(2 * NZ, DEVICES_Z * 8)),
-        inv_z=f(inv_z.reshape(DEVICES_Z * 8, NZ)),
+        inv_z=f(sz),
         lam=f(packed),
         lam_full=f(np.tile(full, (1, 4))),
         lam_x=f(np.tile(coarse_rate * ex[:, None], (1, 128))),
@@ -98,11 +96,30 @@
     return total + pltpu.roll(f, width, 1) + pltpu.roll(f, CY - width, 1)
 
 
-def coarse_kernel(field_ref, strain_ref, fwd_x_ref, fwd_y_ref, coarse_ref, sums):
+def coarse_kernel(
+    field_hbm, strain_hbm, fwd_x_hbm, fwd_y_hbm, coarse_ref,
+    field_ref, strain_ref, fwd_x_ref, fwd_y_ref, sums, sem,
+):
     near = diffusion * kernel_near
     far = diffusion * kernel_far
 
+    def arrays(q):
+        planes = pl.ds(COARSEN * q, COARSEN)
+        return [
+            pltpu.make_async_copy(field_hbm.at[:, planes], field_ref.at[:, planes], sem.at[q, 0]),
+            pltpu.make_async_copy(strain_hbm.at[:, planes], strain_ref.at[:, planes], sem.at[q, 1]),
+        ]
+
+    tables = [
+        pltpu.make_async_copy(fwd_x_hbm, fwd_x_ref, sem.at[2, 0]),
+        pltpu.make_async_copy(fwd_y_hbm, fwd_y_ref, sem.at[2, 1]),
+    ]
+    for copy in arrays(0) + arrays(1) + tables:
+        copy.start()
+
     def block(q, _):
+        for copy in arrays(q):
+            copy.wait()
         basis = [None] * 3
         stretch = [None] * 3
         for k in range(COARSEN):
@@ -115,10 +132,9 @@
                 stretch[c] = acc if k == 0 else stretch[c] + acc
                 basis[c] = comps[c] if k == 0 else basis[c] + comps[c]
         for c in range(3):
-            lanes = slice(c * CY, (c + 1) * CY)
             total = basis[c]
-            sums[q, :, lanes] = total
-            sums[2 + q, :, lanes] = (
+            sums[q, c] = total
+            sums[2 + q, c] = (
                 (1.0 - 4.0 * (near + far)) * total
                 + stretch[c]
                 + near * around(total, 1)
@@ -128,15 +144,22 @@
 
     lax.fori_loop(0, 2, block, 0)
     for c in range(3):
-        lanes = slice(c * CY, (c + 1) * CY)
         low = [diffusion * field_ref[c, 4 * q] + far * field_ref[c, 4 * q + 1] for q in range(2)]
         high = [diffusion * field_ref[c, 4 * q + 3] + far * field_ref[c, 4 * q + 2] for q in range(2)]
         middle = low[1] - high[0]
-        sums[2, :, lanes] += middle - low[0]
-        sums[3, :, lanes] -= middle + high[1]
-        sums[4, :, lanes] = low[0]
-        sums[5, :, lanes] = high[1]
-    along_x = [dot(fwd_x_ref[...], sums[q]) for q in range(6)]
+        sums[2, c] += middle - low[0]
+        sums[3, c] -= middle + high[1]
+        sums[4, c] = low[0]
+        sums[5, c] = high[1]
+    for copy in tables:
+        copy.wait()
+    along_x = []
+    for q in range(6):
+        wide = []
+        for c in range(3):
+            rows = [sums[q, c, pl.ds(k, NX, stride=COARSEN), :] for k in range(COARSEN)]
+            wide.append((rows[0] + rows[1]) + (rows[2] + rows[3]))
+        along_x.append(dot(fwd_x_ref[...], jnp.concatenate(wide, axis=1)))
     modes = dot(jnp.concatenate(along_x, axis=0), fwd_y_ref[...])
     for q in range(6):
         coarse_ref[:, q, :] = modes[NX * q : NX * (q + 1)]
@@ -306,7 +329,9 @@
     rest = jnp.zeros((8, 128), jnp.float32)
     for c in range(3):
         rest = jnp.where(group == c, pltpu.roll(tiles[c], (32 * c - 96) % 128, 1), rest)
-    out_ref[...] = dot(inv_z_ref[...], jnp.concatenate(tiles + [rest], axis=0))
+    planes = dot(inv_z_ref[...], jnp.concatenate(tiles + [rest], axis=0))
+    for s in range(DEVICES_Z):
+        out_ref[s] = planes[2 * s : 2 * s + 2]
 
 
 def pair_kernel(mine_ref, other_ref, out_ref):
@@ -370,8 +395,15 @@
     coarse = call(
         coarse_kernel,
         near_array(NX, 8, 128),
-        [VMEM] * 4,
-        [pltpu.VMEM((6, CX, 3 * CY), jnp.float32)],
+        [HBM] * 4,
+        [
+            pltpu.VMEM(field.shape, jnp.float32),
+            pltpu.VMEM(rates.shape, jnp.bfloat16),
+            pltpu.VMEM((NX, NX), jnp.float32),
+            pltpu.VMEM((3 * CY, 128), jnp.float32),
+            pltpu.VMEM((6, 3, CX, CY), jnp.float32),
+            pltpu.SemaphoreType.DMA((3, 2)),
+        ],
     )(field, rates, con["fwd_x"], con["wide_fwd_y"])
     coarse = lax.all_to_all(coarse, "space", 0, 0, tiled=True)
     mine = call(depth_kernel, near_array(SLICES, 2 * ROWS, 128), [VMEM] * 4)(
@@ -393,10 +425,10 @@
     )
     groups = [list(range(0, count, 2)), list(range(1, count, 2))]
     shares = lax.all_to_all(pair, "space", 0, 0, axis_index_groups=groups, tiled=True)
-    carried = call(solve_kernel, near_array(128, 128), [VMEM] * 5)(
+    carried = call(solve_kernel, near_array(DEVICES_Z, 2, 128), [VMEM] * 5)(
         fast(shares), fast(every), con["inv_z"], con["lam"], con["lam_x"]
     )
-    carried = lax.all_to_all(carried.reshape(DEVICES_Z, 8, 128), "space", 0, 0, tiled=True)
+    carried = lax.all_to_all(carried, "space", 0, 0, tiled=True)
     corrected = call(
         finish_kernel,
         far_array(*field.shape),

time: 70.2 us -> 69.3 us (0.987)
  no operation moved by 1% of the time
where the time goes in v3:
time: 69.3 us; the launch traced here: 68.8 us
  blocking collectives  33.7 us (49%)
  starting transfers between devices  15.6 us (23%)
  Pallas kernels  11.6 us (17%)
  waiting for transfers between devices  7.66 us (11%)
    all_to_all x1, blocking collectives, local(): coarse = lax.all_to_all(coarse, 'space', 0, 0, tiled=True)  17.7 us
    all_to_all x1, blocking collectives, local(): every = lax.all_to_all(mine, 'tm', 0, 0, tiled=True)  16 us
    all_to_all x1, starting transfers between devices, local(): carried = lax.all_to_all(carried, 'space', 0, 0, tiled=True)  4.87 us
    all_to_all x1, waiting for transfers between devices, local(): carried = lax.all_to_all(carried, 'space', 0, 0, tiled=True)  4.22 us
    ppermute x1, starting transfers between devices, local(): lax.ppermute(later[:, DEPTH - 2:], 'space', [(i, i + 1) for i in range(co...  3.43 us
    all_to_all x1, starting transfers between devices, local(): lax.all_to_all(pair, 'space', 0, 0, axis_index_groups=groups, tiled=True)  3.37 us
    pallas_call x1, Pallas kernels, local(): call(fine_kernel, near_array(*field.shape), [VMEM] * 4)  3.14 us
    all_to_all x1, waiting for transfers between devices, local(): lax.all_to_all(pair, 'space', 0, 0, axis_index_groups=groups, tiled=True)  2.6 us
  transfers between devices with their start and end apart: 5, of which 3 were waited for; matrix products, arithmetic and copies ran while one was open for 0% of the time, Pallas kernels for 8%

profile of v3, /device:TPU:1, one launch (start us, length us, event | category | flops | bytes accessed | tf_op | source)
XLA Modules:
  0.0 68.8 jit_solution(6977930695651618978)
XLA Ops:
  0.0 2.5 %shard_map.109 = f32[16,8,128]{2,1,0:T(8,128)S(1)} custom-call(f32[3,8,64,128]{3,2,1,0:T(8,128)} %bitcast.7, bf16[9,8,64,128]{3,2,1,0:T(8,128)(2,1)} %bitcast.10, f32[16,16]{1,0:T(8,128)} %constant.25.clone.fwd_x_hbm, f32[384,128]{1,0:T(8,128)} %constant.26.clone.fwd_y_hbm), custom_call_target="tpu_custom_call" | custom-call | tf_op jit(solution)/shard_map/pallas_call | solution.py:395
  2.5 0.0 copy-start.2
  2.5 0.0 copy-start.7
  2.5 17.7 %all_to_all.20 = f32[16,8,128]{2,1,0:T(8,128)S(1)} all-to-all(f32[16,8,128]{2,1,0:T(8,128)S(1)} %shard_map.109), channel_id=1, replica_groups=mesh['tm'=16,'space'=16] {'space'}, dimensions={0} | all-to-all | bytes 131072 | tf_op jit(solution)/shard_map/all_to_all | solution.py:408
  20.2 0.0 copy-done.1
  20.2 0.3 shard_map.110
  20.5 0.0 copy-start.5
  20.5 16.0 %all_to_all.21.all_ref = f32[16,48,128]{2,1,0:T(8,128)S(1)} all-to-all(f32[16,48,128]{2,1,0:T(8,128)S(1)} %shard_map.110), channel_id=1, replica_groups=mesh['tm'=16,'space'=16] {'tm'}, dimensions={0} | all-to-all | bytes 786432 | tf_op jit(solution)/shard_map/all_to_all | solution.py:413
  36.6 1.2 %shard_map.112.mine_ref = f32[16,256]{1,0:T(8,128)S(1)} custom-call(f32[768,128]{1,0:T(8,128)S(1)} %bitcast.5, f32[24,128]{1,0:T(8,128)S(1)} %copy-done.2, f32[16,128]{1,0:T(8,128)S(1)} %copy-done.1), custom_call_target="tpu_custom_call" | custom-call | tf_op jit(solution)/shard_map/pallas_call | solution.py:416
  37.7 1.7 %collective-permute-start.2 = (f32[16,256]{1,0:T(8,128)S(1)}, f32[16,256]{1,0:T(8,128)S(1)}, u32[]{:S(2)}, u32[]{:S(2)}) collective-permute-start(f32[16,256]{1,0:T(8,128)S(1)} %shard_map.112.mine_ref), channel_id=1, source_target_pairs={{0,1},{1,0},{2,3},{3,2},{4,5},{5,4},{6,7},{7,6},{8,9},{9,8},{10,11... | collective-permute-start | bytes 49160 | tf_op jit(solution)/shard_map/ppermute | solution.py:422
  39.4 0.8 %collective-permute-done.2.other_ref = f32[16,256]{1,0:T(8,128)S(1)} collective-permute-done((f32[16,256]{1,0:T(8,128)S(1)}, f32[16,256]{1,0:T(8,128)S(1)}, u32[]{:S(2)}, u32[]{:S(2)}) %collective-permute-start.2) | collective-permute-done | bytes 16416 | tf_op jit(solution)/shard_map/ppermute | solution.py:422
  40.2 0.7 shard_map.113
  40.9 3.4 %all-to-all-start.2 = ((f32[8,16,256]{2,1,0:T(8,128)}), f32[8,16,256]{2,1,0:T(8,128)S(1)}, u32[]{:S(2)}, u32[]{:S(2)}) async-start(f32[8,16,256]{2,1,0:T(8,128)} %shard_map.113), calls=%async_computation.2 | async-start | bytes 262144 | tf_op jit(solution)/shard_map/all_to_all | solution.py:427
  44.3 2.3 %collective-permute-start.1 = (f32[3,2,64,128]{3,2,1,0:T(8,128)S(1)}, f32[3,2,64,128]{3,2,1,0:T(8,128)S(1)}, u32[]{:S(2)}, u32[]{:S(2)}) collective-permute-start(f32[3,2,64,128]{3,2,1,0:T(8,128)S(1)} %get-tuple-element.9), channel_id=1, source_target_pairs={{1,0},{2,1},{3,2},{4,3},{5,4},{6,5},{7,6},{8,7},{9,8},{10,9},{11,1... | collective-permute-start | bytes 589832 | tf_op jit(solution)/shard_map/ppermute | solution.py:415
  46.6 3.4 %collective-permute-start = (f32[3,2,64,128]{3,2,1,0:T(8,128)S(1)}, f32[3,2,64,128]{3,2,1,0:T(8,128)S(1)}, u32[]{:S(2)}, u32[]{:S(2)}) collective-permute-start(f32[3,2,64,128]{3,2,1,0:T(8,128)S(1)} %get-tuple-element.10), channel_id=1, source_target_pairs={{0,1},{1,2},{2,3},{3,4},{4,5},{5,6},{6,7},{7,8},{8,9},{9,10},{10,1... | collective-permute-start | bytes 589832 | tf_op jit(solution)/shard_map/ppermute | solution.py:414
  50.0 2.6 %all-to-all-done.2.sums_ref = f32[8,16,256]{2,1,0:T(8,128)S(1)} async-done(((f32[8,16,256]{2,1,0:T(8,128)}), f32[8,16,256]{2,1,0:T(8,128)S(1)}, u32[]{:S(2)}, u32[]{:S(2)}) %all-to-all-start.2) | async-done | bytes 131104 | tf_op jit(solution)/shard_map/all_to_all | solution.py:427
  52.6 2.4 %shard_map.114 = f32[16,2,128]{2,1,0:T(2,128)} custom-call(f32[8,16,256]{2,1,0:T(8,128)S(1)} %all-to-all-done.2.sums_ref, f32[16,48,128]{2,1,0:T(8,128)S(1)} %all_to_all.21.all_ref, f32[32,32]{1,0:T(8,128)S(1)} %copy-done.5, f32[24,128]{1,0:T(8,128)S(1)} %copy-done.2, f32[16,128]{1,0:T(8,128)S(1)} %copy-done.1), custom_call_target="tpu_custom_call" | custom-call | tf_op jit(solution)/shard_map/pallas_call | solution.py:428
  55.1 4.9 %all-to-all-start.3 = ((f32[16,2,128]{2,1,0:T(2,128)}), f32[16,2,128]{2,1,0:T(2,128)S(1)}, u32[]{:S(2)}, u32[]{:S(2)}) async-start(f32[16,2,128]{2,1,0:T(2,128)} %shard_map.114), calls=%async_computation.3 | async-start | bytes 32768 | tf_op jit(solution)/shard_map/all_to_all | solution.py:431
  60.0 0.0 copy-start.3
  60.0 0.0 collective-permute-done.1.above_ref
  60.0 0.0 collective-permute-done.below_ref
  60.0 3.1 %shard_map.111.fine_ref = f32[3,8,64,128]{3,2,1,0:T(8,128)S(1)} custom-call(f32[3,8,64,128]{3,2,1,0:T(8,128)} %bitcast.8, bf16[9,8,64,128]{3,2,1,0:T(8,128)(2,1)} %bitcast.11, f32[3,2,64,128]{3,2,1,0:T(8,128)S(1)} %collective-permute-done.below_ref, f32[3,2,64,128]{3,2,1,0:T(8,128)S(1)} %collective-permute-done.1.above_ref), custom_call_target="tpu_custom_call" | custom-call | tf_op jit(solution)/shard_map/pallas_call | solution.py:419
  63.1 4.2 %all-to-all-done.3.modes_ref = f32[16,2,128]{2,1,0:T(2,128)S(1)} async-done(((f32[16,2,128]{2,1,0:T(2,128)}), f32[16,2,128]{2,1,0:T(2,128)S(1)}, u32[]{:S(2)}, u32[]{:S(2)}) %all-to-all-start.3) | async-done | bytes 16416 | tf_op jit(solution)/shard_map/all_to_all | solution.py:431
  67.4 1.5 %shard_map.115 = f32[3,8,64,128]{3,2,1,0:T(8,128)} custom-call(f32[3,8,64,128]{3,2,1,0:T(8,128)S(1)} %shard_map.111.fine_ref, f32[16,2,128]{2,1,0:T(2,128)S(1)} %all-to-all-done.3.modes_ref, f32[64,16]{1,0:T(8,128)S(1)} %copy-done.3, f32[128,384]{1,0:T(8,128)S(1)} %copy-done), custom_call_target="tpu_custom_call" | custom-call | tf_op jit(solution)/shard_map/pallas_call | solution.py:432
  (12 shorter events, 0.0 us)
Async XLA Ops:
  0.0 20.2 %copy-start.1 = (f32[16,128]{1,0:T(8,128)S(1)}, f32[16,128]{1,0:T(8,128)}, u32[]{:S(2)}) copy-start(f32[16,128]{1,0:T(8,128)} %constant.24.clone.lam_x_ref) | copy-start | bytes 24580
  0.0 20.2 %copy-start.4 = (f32[64,128]{1,0:T(8,128)S(1)}, f32[64,128]{1,0:T(8,128)}, u32[]{:S(2)}) copy-start(f32[64,128]{1,0:T(8,128)} %constant.20.clone.fwd_z_ref) | copy-start | bytes 98308
  0.0 20.2 %copy-start.6 = (f32[32,128]{1,0:T(8,128)S(1)}, f32[32,128]{1,0:T(8,128)}, u32[]{:S(2)}) copy-start(f32[32,128]{1,0:T(8,128)} %constant.23.clone.lam_ref) | copy-start | bytes 49156
  2.5 34.1 %copy-start.2 = (f32[24,128]{1,0:T(8,128)S(1)}, f32[24,128]{1,0:T(8,128)}, u32[]{:S(2)}) copy-start(f32[24,128]{1,0:T(8,128)} %constant.22.clone.lam_ref) | copy-start | bytes 36868
  2.5 41.8 %copy-start.7 = (f32[1,3,8,64,128]{4,3,2,1,0:T(8,128)S(1)}, f32[1,3,8,64,128]{4,3,2,1,0:T(8,128)}, u32[]{:S(2)}) copy-start(f32[1,3,8,64,128]{4,3,2,1,0:T(8,128)} %param.11) | copy-start | bytes 2359300
  20.5 32.1 %copy-start.5 = (f32[32,32]{1,0:T(8,128)S(1)}, f32[32,32]{1,0:T(8,128)}, u32[]{:S(2)}) copy-start(f32[32,32]{1,0:T(8,128)} %constant.21.clone.inv_z_ref) | copy-start | bytes 12292
  37.7 2.5 %collective-permute-start.2 = (f32[16,256]{1,0:T(8,128)S(1)}, f32[16,256]{1,0:T(8,128)S(1)}, u32[]{:S(2)}, u32[]{:S(2)}) collective-permute-start(f32[16,256]{1,0:T(8,128)S(1)} %shard_map.112.mine_ref), channel_id=1, source_target_pairs={{0,1},{1,0},{2,3},{3,2},{4,5},{5,4},{6,7},{7,6},{8,9},{9,8},{10,11... | collective-permute-start | bytes 49160 | tf_op jit(solution)/shard_map/ppermute | solution.py:422
  40.9 11.7 %all-to-all-start.2 = ((f32[8,16,256]{2,1,0:T(8,128)}), f32[8,16,256]{2,1,0:T(8,128)S(1)}, u32[]{:S(2)}, u32[]{:S(2)}) async-start(f32[8,16,256]{2,1,0:T(8,128)} %shard_map.113), calls=%async_computation.2 | async-start | bytes 262144 | tf_op jit(solution)/shard_map/all_to_all | solution.py:427
  44.3 15.6 %collective-permute-start.1 = (f32[3,2,64,128]{3,2,1,0:T(8,128)S(1)}, f32[3,2,64,128]{3,2,1,0:T(8,128)S(1)}, u32[]{:S(2)}, u32[]{:S(2)}) collective-permute-start(f32[3,2,64,128]{3,2,1,0:T(8,128)S(1)} %get-tuple-element.9), channel_id=1, source_target_pairs={{1,0},{2,1},{3,2},{4,3},{5,4},{6,5},{7,6},{8,7},{9,8},{10,9},{11,1... | collective-permute-start | bytes 589832 | tf_op jit(solution)/shard_map/ppermute | solution.py:415
  46.6 13.4 %collective-permute-start = (f32[3,2,64,128]{3,2,1,0:T(8,128)S(1)}, f32[3,2,64,128]{3,2,1,0:T(8,128)S(1)}, u32[]{:S(2)}, u32[]{:S(2)}) collective-permute-start(f32[3,2,64,128]{3,2,1,0:T(8,128)S(1)} %get-tuple-element.10), channel_id=1, source_target_pairs={{0,1},{1,2},{2,3},{3,4},{4,5},{5,6},{6,7},{7,8},{8,9},{9,10},{10,1... | collective-permute-start | bytes 589832 | tf_op jit(solution)/shard_map/ppermute | solution.py:414
  55.1 12.3 %all-to-all-start.3 = ((f32[16,2,128]{2,1,0:T(2,128)}), f32[16,2,128]{2,1,0:T(2,128)S(1)}, u32[]{:S(2)}, u32[]{:S(2)}) async-start(f32[16,2,128]{2,1,0:T(2,128)} %shard_map.114), calls=%async_computation.3 | async-start | bytes 32768 | tf_op jit(solution)/shard_map/all_to_all | solution.py:431
  59.9 7.4 %copy-start = (f32[128,384]{1,0:T(8,128)S(1)}, f32[128,384]{1,0:T(8,128)}, u32[]{:S(2)}) copy-start(f32[128,384]{1,0:T(8,128)} %constant.19.clone.inv_y_ref) | copy-start | bytes 589828
  60.0 7.4 %copy-start.3 = (f32[64,16]{1,0:T(8,128)S(1)}, f32[64,16]{1,0:T(8,128)}, u32[]{:S(2)}) copy-start(f32[64,16]{1,0:T(8,128)} %constant.18.clone.inv_x_ref) | copy-start | bytes 12292

commit v4 on v3

--- a/solution.py
+++ b/solution.py
@@ -85,6 +85,19 @@
     return lax.dot_general(
         a, b, (dims, ((), ())), precision=HIGH, preferred_element_type=jnp.float32
     )
+
+
+def halves(x):
+    high = x.astype(jnp.bfloat16)
+    return high, (x - high.astype(jnp.float32)).astype(jnp.bfloat16)
+
+
+def dot_halves(a, b, dims=((1,), (0,))):
+    def part(x, y):
+        return lax.dot_general(x, y, (dims, ((), ())), preferred_element_type=jnp.float32)
+
+    (a_high, a_low), (b_high, b_low) = halves(a), halves(b)
+    return part(a_high, b_high) + (part(a_high, b_low) + part(a_low, b_high))
 
 
 def iota(shape, dim):
@@ -329,7 +342,7 @@
     rest = jnp.zeros((8, 128), jnp.float32)
     for c in range(3):
         rest = jnp.where(group == c, pltpu.roll(tiles[c], (32 * c - 96) % 128, 1), rest)
-    planes = dot(inv_z_ref[...], jnp.concatenate(tiles + [rest], axis=0))
+    planes = dot_halves(inv_z_ref[...], jnp.concatenate(tiles + [rest], axis=0))
     for s in range(DEVICES_Z):
         out_ref[s] = planes[2 * s : 2 * s + 2]
 
@@ -343,7 +356,7 @@
 def finish_kernel(fine_ref, modes_ref, inv_x_ref, inv_y_ref, out_hbm, out_ref, sem):
     copies = []
     for q in range(2):
-        both = dot(dot(inv_x_ref[...], modes_ref[:, q, :]), inv_y_ref[...])
+        both = dot_halves(dot_halves(inv_x_ref[...], modes_ref[:, q, :]), inv_y_ref[...])
         for c in range(3):
             carried = both[:, c * CY : (c + 1) * CY]
             for k in range(COARSEN):

time: 69.3 us -> 69 us (level)
  no operation moved by 1% of the time
where the time goes in v4:
time: 69 us; the launch traced here: 68.6 us
  blocking collectives  33.7 us (49%)
  starting transfers between devices  15.6 us (23%)
  Pallas kernels  11.4 us (17%)
  waiting for transfers between devices  7.66 us (11%)
    all_to_all x1, blocking collectives, local(): coarse = lax.all_to_all(coarse, 'space', 0, 0, tiled=True)  17.7 us
    all_to_all x1, blocking collectives, local(): every = lax.all_to_all(mine, 'tm', 0, 0, tiled=True)  16 us
    all_to_all x1, starting transfers between devices, local(): carried = lax.all_to_all(carried, 'space', 0, 0, tiled=True)  4.87 us
    all_to_all x1, waiting for transfers between devices, local(): carried = lax.all_to_all(carried, 'space', 0, 0, tiled=True)  4.22 us
    ppermute x1, starting transfers between devices, local(): lax.ppermute(later[:, DEPTH - 2:], 'space', [(i, i + 1) for i in range(co...  3.43 us
    all_to_all x1, starting transfers between devices, local(): lax.all_to_all(pair, 'space', 0, 0, axis_index_groups=groups, tiled=True)  3.37 us
    pallas_call x1, Pallas kernels, local(): call(fine_kernel, near_array(*field.shape), [VMEM] * 4)  3.14 us
    all_to_all x1, waiting for transfers between devices, local(): lax.all_to_all(pair, 'space', 0, 0, axis_index_groups=groups, tiled=True)  2.6 us
  transfers between devices with their start and end apart: 5, of which 3 were waited for; matrix products, arithmetic and copies ran while one was open for 0% of the time, Pallas kernels for 8%

profile of v4, /device:TPU:1, one launch (start us, length us, event | category | flops | bytes accessed | tf_op | source)
XLA Modules:
  0.0 68.6 jit_solution(5793406246592565999)
XLA Ops:
  0.0 2.5 %shard_map.109 = f32[16,8,128]{2,1,0:T(8,128)S(1)} custom-call(f32[3,8,64,128]{3,2,1,0:T(8,128)} %bitcast.7, bf16[9,8,64,128]{3,2,1,0:T(8,128)(2,1)} %bitcast.10, f32[16,16]{1,0:T(8,128)} %constant.25.clone.fwd_x_hbm, f32[384,128]{1,0:T(8,128)} %constant.26.clone.fwd_y_hbm), custom_call_target="tpu_custom_call" | custom-call | tf_op jit(solution)/shard_map/pallas_call | solution.py:408
  2.5 0.0 copy-start.2
  2.5 0.0 copy-start.7
  2.5 17.7 %all_to_all.20 = f32[16,8,128]{2,1,0:T(8,128)S(1)} all-to-all(f32[16,8,128]{2,1,0:T(8,128)S(1)} %shard_map.109), channel_id=1, replica_groups=mesh['tm'=16,'space'=16] {'space'}, dimensions={0} | all-to-all | bytes 131072 | tf_op jit(solution)/shard_map/all_to_all | solution.py:421
  20.2 0.3 shard_map.110
  20.5 0.0 copy-start.5
  20.5 16.0 %all_to_all.21.all_ref = f32[16,48,128]{2,1,0:T(8,128)S(1)} all-to-all(f32[16,48,128]{2,1,0:T(8,128)S(1)} %shard_map.110), channel_id=1, replica_groups=mesh['tm'=16,'space'=16] {'tm'}, dimensions={0} | all-to-all | bytes 786432 | tf_op jit(solution)/shard_map/all_to_all | solution.py:426
  36.6 1.2 %shard_map.112.mine_ref = f32[16,256]{1,0:T(8,128)S(1)} custom-call(f32[768,128]{1,0:T(8,128)S(1)} %bitcast.5, f32[24,128]{1,0:T(8,128)S(1)} %copy-done.2, f32[16,128]{1,0:T(8,128)S(1)} %copy-done.1), custom_call_target="tpu_custom_call" | custom-call | tf_op jit(solution)/shard_map/pallas_call | solution.py:429
  37.7 1.7 %collective-permute-start.2 = (f32[16,256]{1,0:T(8,128)S(1)}, f32[16,256]{1,0:T(8,128)S(1)}, u32[]{:S(2)}, u32[]{:S(2)}) collective-permute-start(f32[16,256]{1,0:T(8,128)S(1)} %shard_map.112.mine_ref), channel_id=1, source_target_pairs={{0,1},{1,0},{2,3},{3,2},{4,5},{5,4},{6,7},{7,6},{8,9},{9,8},{10,11... | collective-permute-start | bytes 49160 | tf_op jit(solution)/shard_map/ppermute | solution.py:435
  39.4 0.8 %collective-permute-done.2.other_ref = f32[16,256]{1,0:T(8,128)S(1)} collective-permute-done((f32[16,256]{1,0:T(8,128)S(1)}, f32[16,256]{1,0:T(8,128)S(1)}, u32[]{:S(2)}, u32[]{:S(2)}) %collective-permute-start.2) | collective-permute-done | bytes 16416 | tf_op jit(solution)/shard_map/ppermute | solution.py:435
  40.2 0.7 shard_map.113
  40.9 3.4 %all-to-all-start.2 = ((f32[8,16,256]{2,1,0:T(8,128)}), f32[8,16,256]{2,1,0:T(8,128)S(1)}, u32[]{:S(2)}, u32[]{:S(2)}) async-start(f32[8,16,256]{2,1,0:T(8,128)} %shard_map.113), calls=%async_computation.2 | async-start | bytes 262144 | tf_op jit(solution)/shard_map/all_to_all | solution.py:440
  44.3 2.3 %collective-permute-start.1 = (f32[3,2,64,128]{3,2,1,0:T(8,128)S(1)}, f32[3,2,64,128]{3,2,1,0:T(8,128)S(1)}, u32[]{:S(2)}, u32[]{:S(2)}) collective-permute-start(f32[3,2,64,128]{3,2,1,0:T(8,128)S(1)} %get-tuple-element.9), channel_id=1, source_target_pairs={{1,0},{2,1},{3,2},{4,3},{5,4},{6,5},{7,6},{8,7},{9,8},{10,9},{11,1... | collective-permute-start | bytes 589832 | tf_op jit(solution)/shard_map/ppermute | solution.py:428
  46.6 3.4 %collective-permute-start = (f32[3,2,64,128]{3,2,1,0:T(8,128)S(1)}, f32[3,2,64,128]{3,2,1,0:T(8,128)S(1)}, u32[]{:S(2)}, u32[]{:S(2)}) collective-permute-start(f32[3,2,64,128]{3,2,1,0:T(8,128)S(1)} %get-tuple-element.10), channel_id=1, source_target_pairs={{0,1},{1,2},{2,3},{3,4},{4,5},{5,6},{6,7},{7,8},{8,9},{9,10},{10,1... | collective-permute-start | bytes 589832 | tf_op jit(solution)/shard_map/ppermute | solution.py:427
  50.0 2.6 %all-to-all-done.2.sums_ref = f32[8,16,256]{2,1,0:T(8,128)S(1)} async-done(((f32[8,16,256]{2,1,0:T(8,128)}), f32[8,16,256]{2,1,0:T(8,128)S(1)}, u32[]{:S(2)}, u32[]{:S(2)}) %all-to-all-start.2) | async-done | bytes 131104 | tf_op jit(solution)/shard_map/all_to_all | solution.py:440
  52.6 2.4 %shard_map.114 = f32[16,2,128]{2,1,0:T(2,128)} custom-call(f32[8,16,256]{2,1,0:T(8,128)S(1)} %all-to-all-done.2.sums_ref, f32[16,48,128]{2,1,0:T(8,128)S(1)} %all_to_all.21.all_ref, f32[32,32]{1,0:T(8,128)S(1)} %copy-done.5, f32[24,128]{1,0:T(8,128)S(1)} %copy-done.2, f32[16,128]{1,0:T(8,128)S(1)} %copy-done.1), custom_call_target="tpu_custom_call" | custom-call | tf_op jit(solution)/shard_map/pallas_call | solution.py:441
  55.0 4.9 %all-to-all-start.3 = ((f32[16,2,128]{2,1,0:T(2,128)}), f32[16,2,128]{2,1,0:T(2,128)S(1)}, u32[]{:S(2)}, u32[]{:S(2)}) async-start(f32[16,2,128]{2,1,0:T(2,128)} %shard_map.114), calls=%async_computation.3 | async-start | bytes 32768 | tf_op jit(solution)/shard_map/all_to_all | solution.py:444
  59.9 0.0 copy-start.3
  59.9 0.0 collective-permute-done.1.above_ref
  59.9 0.0 collective-permute-done.below_ref
  59.9 3.1 %shard_map.111.fine_ref = f32[3,8,64,128]{3,2,1,0:T(8,128)S(1)} custom-call(f32[3,8,64,128]{3,2,1,0:T(8,128)} %bitcast.8, bf16[9,8,64,128]{3,2,1,0:T(8,128)(2,1)} %bitcast.11, f32[3,2,64,128]{3,2,1,0:T(8,128)S(1)} %collective-permute-done.below_ref, f32[3,2,64,128]{3,2,1,0:T(8,128)S(1)} %collective-permute-done.1.above_ref), custom_call_target="tpu_custom_call" | custom-call | tf_op jit(solution)/shard_map/pallas_call | solution.py:432
  63.1 4.2 %all-to-all-done.3.modes_ref = f32[16,2,128]{2,1,0:T(2,128)S(1)} async-done(((f32[16,2,128]{2,1,0:T(2,128)}), f32[16,2,128]{2,1,0:T(2,128)S(1)}, u32[]{:S(2)}, u32[]{:S(2)}) %all-to-all-start.3) | async-done | bytes 16416 | tf_op jit(solution)/shard_map/all_to_all | solution.py:444
  67.3 0.0 copy-done
  67.3 1.3 %shard_map.115 = f32[3,8,64,128]{3,2,1,0:T(8,128)} custom-call(f32[3,8,64,128]{3,2,1,0:T(8,128)S(1)} %shard_map.111.fine_ref, f32[16,2,128]{2,1,0:T(2,128)S(1)} %all-to-all-done.3.modes_ref, f32[64,16]{1,0:T(8,128)S(1)} %copy-done.3, f32[128,384]{1,0:T(8,128)S(1)} %copy-done), custom_call_target="tpu_custom_call" | custom-call | tf_op jit(solution)/shard_map/pallas_call | solution.py:445
  (12 shorter events, 0.0 us)
Async XLA Ops:
  0.0 20.2 %copy-start.1 = (f32[16,128]{1,0:T(8,128)S(1)}, f32[16,128]{1,0:T(8,128)}, u32[]{:S(2)}) copy-start(f32[16,128]{1,0:T(8,128)} %constant.24.clone.lam_x_ref) | copy-start | bytes 24580
  0.0 20.2 %copy-start.4 = (f32[64,128]{1,0:T(8,128)S(1)}, f32[64,128]{1,0:T(8,128)}, u32[]{:S(2)}) copy-start(f32[64,128]{1,0:T(8,128)} %constant.20.clone.fwd_z_ref) | copy-start | bytes 98308
  0.0 20.2 %copy-start.6 = (f32[32,128]{1,0:T(8,128)S(1)}, f32[32,128]{1,0:T(8,128)}, u32[]{:S(2)}) copy-start(f32[32,128]{1,0:T(8,128)} %constant.23.clone.lam_ref) | copy-start | bytes 49156
  2.5 34.1 %copy-start.2 = (f32[24,128]{1,0:T(8,128)S(1)}, f32[24,128]{1,0:T(8,128)}, u32[]{:S(2)}) copy-start(f32[24,128]{1,0:T(8,128)} %constant.22.clone.lam_ref) | copy-start | bytes 36868
  2.5 41.8 %copy-start.7 = (f32[1,3,8,64,128]{4,3,2,1,0:T(8,128)S(1)}, f32[1,3,8,64,128]{4,3,2,1,0:T(8,128)}, u32[]{:S(2)}) copy-start(f32[1,3,8,64,128]{4,3,2,1,0:T(8,128)} %param.11) | copy-start | bytes 2359300
  20.5 32.1 %copy-start.5 = (f32[32,32]{1,0:T(8,128)S(1)}, f32[32,32]{1,0:T(8,128)}, u32[]{:S(2)}) copy-start(f32[32,32]{1,0:T(8,128)} %constant.21.clone.inv_z_ref) | copy-start | bytes 12292
  37.7 2.5 %collective-permute-start.2 = (f32[16,256]{1,0:T(8,128)S(1)}, f32[16,256]{1,0:T(8,128)S(1)}, u32[]{:S(2)}, u32[]{:S(2)}) collective-permute-start(f32[16,256]{1,0:T(8,128)S(1)} %shard_map.112.mine_ref), channel_id=1, source_target_pairs={{0,1},{1,0},{2,3},{3,2},{4,5},{5,4},{6,7},{7,6},{8,9},{9,8},{10,11... | collective-permute-start | bytes 49160 | tf_op jit(solution)/shard_map/ppermute | solution.py:435
  40.9 11.7 %all-to-all-start.2 = ((f32[8,16,256]{2,1,0:T(8,128)}), f32[8,16,256]{2,1,0:T(8,128)S(1)}, u32[]{:S(2)}, u32[]{:S(2)}) async-start(f32[8,16,256]{2,1,0:T(8,128)} %shard_map.113), calls=%async_computation.2 | async-start | bytes 262144 | tf_op jit(solution)/shard_map/all_to_all | solution.py:440
  44.3 15.6 %collective-permute-start.1 = (f32[3,2,64,128]{3,2,1,0:T(8,128)S(1)}, f32[3,2,64,128]{3,2,1,0:T(8,128)S(1)}, u32[]{:S(2)}, u32[]{:S(2)}) collective-permute-start(f32[3,2,64,128]{3,2,1,0:T(8,128)S(1)} %get-tuple-element.9), channel_id=1, source_target_pairs={{1,0},{2,1},{3,2},{4,3},{5,4},{6,5},{7,6},{8,7},{9,8},{10,9},{11,1... | collective-permute-start | bytes 589832 | tf_op jit(solution)/shard_map/ppermute | solution.py:428
  46.6 13.3 %collective-permute-start = (f32[3,2,64,128]{3,2,1,0:T(8,128)S(1)}, f32[3,2,64,128]{3,2,1,0:T(8,128)S(1)}, u32[]{:S(2)}, u32[]{:S(2)}) collective-permute-start(f32[3,2,64,128]{3,2,1,0:T(8,128)S(1)} %get-tuple-element.10), channel_id=1, source_target_pairs={{0,1},{1,2},{2,3},{3,4},{4,5},{5,6},{6,7},{7,8},{8,9},{9,10},{10,1... | collective-permute-start | bytes 589832 | tf_op jit(solution)/shard_map/ppermute | solution.py:427
  55.0 12.3 %all-to-all-start.3 = ((f32[16,2,128]{2,1,0:T(2,128)}), f32[16,2,128]{2,1,0:T(2,128)S(1)}, u32[]{:S(2)}, u32[]{:S(2)}) async-start(f32[16,2,128]{2,1,0:T(2,128)} %shard_map.114), calls=%async_computation.3 | async-start | bytes 32768 | tf_op jit(solution)/shard_map/all_to_all | solution.py:444
  59.9 7.4 %copy-start = (f32[128,384]{1,0:T(8,128)S(1)}, f32[128,384]{1,0:T(8,128)}, u32[]{:S(2)}) copy-start(f32[128,384]{1,0:T(8,128)} %constant.19.clone.inv_y_ref) | copy-start | bytes 589828
  59.9 7.4 %copy-start.3 = (f32[64,16]{1,0:T(8,128)S(1)}, f32[64,16]{1,0:T(8,128)}, u32[]{:S(2)}) copy-start(f32[64,16]{1,0:T(8,128)} %constant.18.clone.inv_x_ref) | copy-start | bytes 12292

commit v5 on v3

--- a/solution.py
+++ b/solution.py
@@ -313,11 +313,12 @@
             acc_one, acc_two = grown_one, grown_two
     weights = jnp.concatenate(weights, axis=0)
     tiles = []
+    defects = [all_ref[:, ROWS + 8 * g : ROWS + 8 * g + 8, :].reshape(128, 128) for g in range(3)]
+    every_term = dot(weights, jnp.concatenate(defects, axis=1))
     for g in range(3):
         rows = slice(8 * g, 8 * g + 8)
         lam = lam_ref[rows] + shift
-        d = all_ref[:, ROWS + 8 * g : ROWS + 8 * g + 8, :].reshape(128, 128)
-        terms = dot(weights, d)
+        terms = every_term[:, 128 * g : 128 * g + 128]
         b0 = all_ref[0, rows, :]
         value = terms[0:8] + lam * b0
         for k in range(1, SLICES):
@@ -342,8 +343,11 @@
 
 def finish_kernel(fine_ref, modes_ref, inv_x_ref, inv_y_ref, out_hbm, out_ref, sem):
     copies = []
+    wide = dot(inv_x_ref[...], jnp.concatenate([modes_ref[:, q, :] for q in range(2)], axis=1))
+    tall = jnp.concatenate([wide[:, :128], wide[:, 128:]], axis=0)
+    blocks = dot(tall, inv_y_ref[...])
     for q in range(2):
-        both = dot(dot(inv_x_ref[...], modes_ref[:, q, :]), inv_y_ref[...])
+        both = blocks[CX * q : CX * q + CX]
         for c in range(3):
             carried = both[:, c * CY : (c + 1) * CY]
             for k in range(COARSEN):

time: 69.3 us -> 69.3 us (level)
  no operation moved by 1% of the time
where the time goes in v5:
time: 69.3 us; the launch traced here: 68.8 us
  blocking collectives  33.7 us (49%)
  starting transfers between devices  15.6 us (23%)
  Pallas kernels  11.6 us (17%)
  waiting for transfers between devices  7.66 us (11%)
    all_to_all x1, blocking collectives, local(): coarse = lax.all_to_all(coarse, 'space', 0, 0, tiled=True)  17.7 us
    all_to_all x1, blocking collectives, local(): every = lax.all_to_all(mine, 'tm', 0, 0, tiled=True)  16 us
    all_to_all x1, starting transfers between devices, local(): carried = lax.all_to_all(carried, 'space', 0, 0, tiled=True)  4.87 us
    all_to_all x1, waiting for transfers between devices, local(): carried = lax.all_to_all(carried, 'space', 0, 0, tiled=True)  4.22 us
    ppermute x1, starting transfers between devices, local(): lax.ppermute(later[:, DEPTH - 2:], 'space', [(i, i + 1) for i in range(co...  3.43 us
    all_to_all x1, starting transfers between devices, local(): lax.all_to_all(pair, 'space', 0, 0, axis_index_groups=groups, tiled=True)  3.37 us
    pallas_call x1, Pallas kernels, local(): call(fine_kernel, near_array(*field.shape), [VMEM] * 4)  3.14 us
    all_to_all x1, waiting for transfers between devices, local(): lax.all_to_all(pair, 'space', 0, 0, axis_index_groups=groups, tiled=True)  2.6 us
  transfers between devices with their start and end apart: 5, of which 3 were waited for; matrix products, arithmetic and copies ran while one was open for 0% of the time, Pallas kernels for 8%

profile of v5, /device:TPU:1, one launch (start us, length us, event | category | flops | bytes accessed | tf_op | source)
XLA Modules:
  0.0 68.8 jit_solution(13095964325954313141)
XLA Ops:
  0.0 2.5 %shard_map.109 = f32[16,8,128]{2,1,0:T(8,128)S(1)} custom-call(f32[3,8,64,128]{3,2,1,0:T(8,128)} %bitcast.7, bf16[9,8,64,128]{3,2,1,0:T(8,128)(2,1)} %bitcast.10, f32[16,16]{1,0:T(8,128)} %constant.25.clone.fwd_x_hbm, f32[384,128]{1,0:T(8,128)} %constant.26.clone.fwd_y_hbm), custom_call_target="tpu_custom_call" | custom-call | tf_op jit(solution)/shard_map/pallas_call | solution.py:399
  2.5 0.0 copy-start.2
  2.5 0.0 copy-start.7
  2.5 17.7 %all_to_all.20 = f32[16,8,128]{2,1,0:T(8,128)S(1)} all-to-all(f32[16,8,128]{2,1,0:T(8,128)S(1)} %shard_map.109), channel_id=1, replica_groups=mesh['tm'=16,'space'=16] {'space'}, dimensions={0} | all-to-all | bytes 131072 | tf_op jit(solution)/shard_map/all_to_all | solution.py:412
  20.2 0.0 copy-done.1
  20.2 0.3 shard_map.110
  20.5 0.0 copy-start.5
  20.5 16.0 %all_to_all.21.all_ref = f32[16,48,128]{2,1,0:T(8,128)S(1)} all-to-all(f32[16,48,128]{2,1,0:T(8,128)S(1)} %shard_map.110), channel_id=1, replica_groups=mesh['tm'=16,'space'=16] {'tm'}, dimensions={0} | all-to-all | bytes 786432 | tf_op jit(solution)/shard_map/all_to_all | solution.py:417
  36.6 1.2 %shard_map.112.mine_ref = f32[16,256]{1,0:T(8,128)S(1)} custom-call(f32[768,128]{1,0:T(8,128)S(1)} %bitcast.5, f32[24,128]{1,0:T(8,128)S(1)} %copy-done.2, f32[16,128]{1,0:T(8,128)S(1)} %copy-done.1), custom_call_target="tpu_custom_call" | custom-call | tf_op jit(solution)/shard_map/pallas_call | solution.py:420
  37.7 1.7 %collective-permute-start.2 = (f32[16,256]{1,0:T(8,128)S(1)}, f32[16,256]{1,0:T(8,128)S(1)}, u32[]{:S(2)}, u32[]{:S(2)}) collective-permute-start(f32[16,256]{1,0:T(8,128)S(1)} %shard_map.112.mine_ref), channel_id=1, source_target_pairs={{0,1},{1,0},{2,3},{3,2},{4,5},{5,4},{6,7},{7,6},{8,9},{9,8},{10,11... | collective-permute-start | bytes 49160 | tf_op jit(solution)/shard_map/ppermute | solution.py:426
  39.4 0.8 %collective-permute-done.2.other_ref = f32[16,256]{1,0:T(8,128)S(1)} collective-permute-done((f32[16,256]{1,0:T(8,128)S(1)}, f32[16,256]{1,0:T(8,128)S(1)}, u32[]{:S(2)}, u32[]{:S(2)}) %collective-permute-start.2) | collective-permute-done | bytes 16416 | tf_op jit(solution)/shard_map/ppermute | solution.py:426
  40.2 0.7 shard_map.113
  40.9 3.4 %all-to-all-start.2 = ((f32[8,16,256]{2,1,0:T(8,128)}), f32[8,16,256]{2,1,0:T(8,128)S(1)}, u32[]{:S(2)}, u32[]{:S(2)}) async-start(f32[8,16,256]{2,1,0:T(8,128)} %shard_map.113), calls=%async_computation.2 | async-start | bytes 262144 | tf_op jit(solution)/shard_map/all_to_all | solution.py:431
  44.3 2.3 %collective-permute-start.1 = (f32[3,2,64,128]{3,2,1,0:T(8,128)S(1)}, f32[3,2,64,128]{3,2,1,0:T(8,128)S(1)}, u32[]{:S(2)}, u32[]{:S(2)}) collective-permute-start(f32[3,2,64,128]{3,2,1,0:T(8,128)S(1)} %get-tuple-element.9), channel_id=1, source_target_pairs={{1,0},{2,1},{3,2},{4,3},{5,4},{6,5},{7,6},{8,7},{9,8},{10,9},{11,1... | collective-permute-start | bytes 589832 | tf_op jit(solution)/shard_map/ppermute | solution.py:419
  46.6 3.4 %collective-permute-start = (f32[3,2,64,128]{3,2,1,0:T(8,128)S(1)}, f32[3,2,64,128]{3,2,1,0:T(8,128)S(1)}, u32[]{:S(2)}, u32[]{:S(2)}) collective-permute-start(f32[3,2,64,128]{3,2,1,0:T(8,128)S(1)} %get-tuple-element.10), channel_id=1, source_target_pairs={{0,1},{1,2},{2,3},{3,4},{4,5},{5,6},{6,7},{7,8},{8,9},{9,10},{10,1... | collective-permute-start | bytes 589832 | tf_op jit(solution)/shard_map/ppermute | solution.py:418
  50.0 2.6 %all-to-all-done.2.sums_ref = f32[8,16,256]{2,1,0:T(8,128)S(1)} async-done(((f32[8,16,256]{2,1,0:T(8,128)}), f32[8,16,256]{2,1,0:T(8,128)S(1)}, u32[]{:S(2)}, u32[]{:S(2)}) %all-to-all-start.2) | async-done | bytes 131104 | tf_op jit(solution)/shard_map/all_to_all | solution.py:431
  52.6 2.4 %shard_map.114 = f32[16,2,128]{2,1,0:T(2,128)} custom-call(f32[8,16,256]{2,1,0:T(8,128)S(1)} %all-to-all-done.2.sums_ref, f32[16,48,128]{2,1,0:T(8,128)S(1)} %all_to_all.21.all_ref, f32[32,32]{1,0:T(8,128)S(1)} %copy-done.5, f32[24,128]{1,0:T(8,128)S(1)} %copy-done.2, f32[16,128]{1,0:T(8,128)S(1)} %copy-done.1), custom_call_target="tpu_custom_call" | custom-call | tf_op jit(solution)/shard_map/pallas_call | solution.py:432
  55.1 4.9 %all-to-all-start.3 = ((f32[16,2,128]{2,1,0:T(2,128)}), f32[16,2,128]{2,1,0:T(2,128)S(1)}, u32[]{:S(2)}, u32[]{:S(2)}) async-start(f32[16,2,128]{2,1,0:T(2,128)} %shard_map.114), calls=%async_computation.3 | async-start | bytes 32768 | tf_op jit(solution)/shard_map/all_to_all | solution.py:435
  59.9 0.0 copy-start.3
  59.9 0.0 collective-permute-done.1.above_ref
  60.0 0.0 collective-permute-done.below_ref
  60.0 3.1 %shard_map.111.fine_ref = f32[3,8,64,128]{3,2,1,0:T(8,128)S(1)} custom-call(f32[3,8,64,128]{3,2,1,0:T(8,128)} %bitcast.8, bf16[9,8,64,128]{3,2,1,0:T(8,128)(2,1)} %bitcast.11, f32[3,2,64,128]{3,2,1,0:T(8,128)S(1)} %collective-permute-done.below_ref, f32[3,2,64,128]{3,2,1,0:T(8,128)S(1)} %collective-permute-done.1.above_ref), custom_call_target="tpu_custom_call" | custom-call | tf_op jit(solution)/shard_map/pallas_call | solution.py:423
  63.1 4.2 %all-to-all-done.3.modes_ref = f32[16,2,128]{2,1,0:T(2,128)S(1)} async-done(((f32[16,2,128]{2,1,0:T(2,128)}), f32[16,2,128]{2,1,0:T(2,128)S(1)}, u32[]{:S(2)}, u32[]{:S(2)}) %all-to-all-start.3) | async-done | bytes 16416 | tf_op jit(solution)/shard_map/all_to_all | solution.py:435
  67.3 1.5 %shard_map.115 = f32[3,8,64,128]{3,2,1,0:T(8,128)} custom-call(f32[3,8,64,128]{3,2,1,0:T(8,128)S(1)} %shard_map.111.fine_ref, f32[16,2,128]{2,1,0:T(2,128)S(1)} %all-to-all-done.3.modes_ref, f32[64,16]{1,0:T(8,128)S(1)} %copy-done.3, f32[128,384]{1,0:T(8,128)S(1)} %copy-done), custom_call_target="tpu_custom_call" | custom-call | tf_op jit(solution)/shard_map/pallas_call | solution.py:436
  (12 shorter events, 0.0 us)
Async XLA Ops:
  0.0 20.2 %copy-start.1 = (f32[16,128]{1,0:T(8,128)S(1)}, f32[16,128]{1,0:T(8,128)}, u32[]{:S(2)}) copy-start(f32[16,128]{1,0:T(8,128)} %constant.24.clone.lam_x_ref) | copy-start | bytes 24580
  0.0 20.2 %copy-start.4 = (f32[64,128]{1,0:T(8,128)S(1)}, f32[64,128]{1,0:T(8,128)}, u32[]{:S(2)}) copy-start(f32[64,128]{1,0:T(8,128)} %constant.20.clone.fwd_z_ref) | copy-start | bytes 98308
  0.0 20.2 %copy-start.6 = (f32[32,128]{1,0:T(8,128)S(1)}, f32[32,128]{1,0:T(8,128)}, u32[]{:S(2)}) copy-start(f32[32,128]{1,0:T(8,128)} %constant.23.clone.lam_ref) | copy-start | bytes 49156
  2.5 34.1 %copy-start.2 = (f32[24,128]{1,0:T(8,128)S(1)}, f32[24,128]{1,0:T(8,128)}, u32[]{:S(2)}) copy-start(f32[24,128]{1,0:T(8,128)} %constant.22.clone.lam_ref) | copy-start | bytes 36868
  2.5 41.8 %copy-start.7 = (f32[1,3,8,64,128]{4,3,2,1,0:T(8,128)S(1)}, f32[1,3,8,64,128]{4,3,2,1,0:T(8,128)}, u32[]{:S(2)}) copy-start(f32[1,3,8,64,128]{4,3,2,1,0:T(8,128)} %param.11) | copy-start | bytes 2359300
  20.5 32.1 %copy-start.5 = (f32[32,32]{1,0:T(8,128)S(1)}, f32[32,32]{1,0:T(8,128)}, u32[]{:S(2)}) copy-start(f32[32,32]{1,0:T(8,128)} %constant.21.clone.inv_z_ref) | copy-start | bytes 12292
  37.7 2.5 %collective-permute-start.2 = (f32[16,256]{1,0:T(8,128)S(1)}, f32[16,256]{1,0:T(8,128)S(1)}, u32[]{:S(2)}, u32[]{:S(2)}) collective-permute-start(f32[16,256]{1,0:T(8,128)S(1)} %shard_map.112.mine_ref), channel_id=1, source_target_pairs={{0,1},{1,0},{2,3},{3,2},{4,5},{5,4},{6,7},{7,6},{8,9},{9,8},{10,11... | collective-permute-start | bytes 49160 | tf_op jit(solution)/shard_map/ppermute | solution.py:426
  40.9 11.7 %all-to-all-start.2 = ((f32[8,16,256]{2,1,0:T(8,128)}), f32[8,16,256]{2,1,0:T(8,128)S(1)}, u32[]{:S(2)}, u32[]{:S(2)}) async-start(f32[8,16,256]{2,1,0:T(8,128)} %shard_map.113), calls=%async_computation.2 | async-start | bytes 262144 | tf_op jit(solution)/shard_map/all_to_all | solution.py:431
  44.3 15.6 %collective-permute-start.1 = (f32[3,2,64,128]{3,2,1,0:T(8,128)S(1)}, f32[3,2,64,128]{3,2,1,0:T(8,128)S(1)}, u32[]{:S(2)}, u32[]{:S(2)}) collective-permute-start(f32[3,2,64,128]{3,2,1,0:T(8,128)S(1)} %get-tuple-element.9), channel_id=1, source_target_pairs={{1,0},{2,1},{3,2},{4,3},{5,4},{6,5},{7,6},{8,7},{9,8},{10,9},{11,1... | collective-permute-start | bytes 589832 | tf_op jit(solution)/shard_map/ppermute | solution.py:419
  46.6 13.4 %collective-permute-start = (f32[3,2,64,128]{3,2,1,0:T(8,128)S(1)}, f32[3,2,64,128]{3,2,1,0:T(8,128)S(1)}, u32[]{:S(2)}, u32[]{:S(2)}) collective-permute-start(f32[3,2,64,128]{3,2,1,0:T(8,128)S(1)} %get-tuple-element.10), channel_id=1, source_target_pairs={{0,1},{1,2},{2,3},{3,4},{4,5},{5,6},{6,7},{7,8},{8,9},{9,10},{10,1... | collective-permute-start | bytes 589832 | tf_op jit(solution)/shard_map/ppermute | solution.py:418
  55.1 12.3 %all-to-all-start.3 = ((f32[16,2,128]{2,1,0:T(2,128)}), f32[16,2,128]{2,1,0:T(2,128)S(1)}, u32[]{:S(2)}, u32[]{:S(2)}) async-start(f32[16,2,128]{2,1,0:T(2,128)} %shard_map.114), calls=%async_computation.3 | async-start | bytes 32768 | tf_op jit(solution)/shard_map/all_to_all | solution.py:435
  59.9 7.4 %copy-start = (f32[128,384]{1,0:T(8,128)S(1)}, f32[128,384]{1,0:T(8,128)}, u32[]{:S(2)}) copy-start(f32[128,384]{1,0:T(8,128)} %constant.19.clone.inv_y_ref) | copy-start | bytes 589828
  59.9 7.4 %copy-start.3 = (f32[64,16]{1,0:T(8,128)S(1)}, f32[64,16]{1,0:T(8,128)}, u32[]{:S(2)}) copy-start(f32[64,16]{1,0:T(8,128)} %constant.18.clone.inv_x_ref) | copy-start | bytes 12292
